TPU v7x, 128 devices: a whole 4x4x4 slice. The times are simulated.
128 devices in a mesh: aa: 16 (over z, x_lo, core), ba: 8 (over y, x_hi).
Axes of the slice: x: 4 (x_hi: 2, x_lo: 2; x = x_hi * 2 + x_lo), y: 4, z: 4, core: 2. Of those that a mesh axis runs over, the one named last changes fastest.
Arguments:
- tensor: bfloat16 [576, 576, 576], P('aa', 'ba'), may hold values from -20 to 20
- trial_x: float32 [576, 24], replicated, may hold values from -0.25 to 0.25
- trial_y: float32 [576, 24], replicated, may hold values from -0.25 to 0.25
Outputs:
- gram_x: float32 [576, 576], P('aa')
- proj_x: float32 [576, 24], P('aa')
- gram_y: float32 [576, 576], P('ba')
- proj_y: float32 [576, 24], P('ba')
All inputs are finite; a program needn't handle non-finite values.
Results may differ from a plain program's by a relative error of at most 0.0003.
Values may be sent and summed in bfloat16 or wider, within the bound.
A program may use at most 192 MiB of HBM per device.

v0:
```python
import jax
import jax.numpy as jnp
from jax import lax
from jax.sharding import PartitionSpec as P


def leg_factor(block, bond_dim):
    row_count = block.shape[0]
    shaped = block.reshape(bond_dim, row_count // bond_dim, block.shape[1], bond_dim)
    products = jnp.einsum("aprk,bprl->akbl", shaped, shaped, preferred_element_type=jnp.float32)
    return products.reshape(row_count, row_count) * (1.0 / bond_dim**3)


def x_factors(blocks, bond_dim):
    x_height, y_width = (blocks.shape[0], blocks.shape[1])
    upper_view = blocks.reshape(x_height, y_width * bond_dim, bond_dim)
    lower_view = jnp.swapaxes(blocks, 2, 3).reshape(x_height, y_width * bond_dim, bond_dim)
    upper_all, lower_all = (
        lax.all_to_all(upper_view, "aa", split_axis=1, concat_axis=0, tiled=True),
        lax.all_to_all(lower_view, "aa", split_axis=1, concat_axis=0, tiled=True),
    )
    return (leg_factor(upper_all, bond_dim), leg_factor(lower_all, bond_dim))


def y_factors(blocks, bond_dim):
    x_height, y_width = (blocks.shape[0], blocks.shape[1])
    upper_view = jnp.transpose(blocks, (1, 0, 2, 3)).reshape(y_width, x_height * bond_dim, bond_dim)
    lower_view = jnp.transpose(blocks, (1, 0, 3, 2)).reshape(y_width, x_height * bond_dim, bond_dim)
    upper_all, lower_all = (
        lax.all_to_all(upper_view, "ba", split_axis=1, concat_axis=0, tiled=True),
        lax.all_to_all(lower_view, "ba", split_axis=1, concat_axis=0, tiled=True),
    )
    return (leg_factor(upper_all, bond_dim), leg_factor(lower_all, bond_dim))


def summed_x(factors):
    return lax.psum((factors[0], factors[1]), ("aa", "ba"))


def summed_y(factors):
    return lax.psum((factors[0], factors[1]), ("aa", "ba"))


def compose(q_up, q_low, bond_dim):
    order = bond_dim * bond_dim
    up_matrix = (
        q_up.reshape(bond_dim, bond_dim, bond_dim, bond_dim)
        .transpose(0, 2, 1, 3)
        .reshape(order, order)
    )
    low_matrix = (
        q_low.reshape(bond_dim, bond_dim, bond_dim, bond_dim)
        .transpose(0, 2, 1, 3)
        .reshape(order, order)
    )
    joined = jnp.dot(
        up_matrix, low_matrix.T, precision=lax.Precision.HIGHEST, preferred_element_type=jnp.float32
    )
    return joined.reshape(bond_dim, bond_dim, bond_dim, bond_dim).transpose(0, 2, 1, 3).reshape(
        order, order
    ) * (1.0 / bond_dim**3)


def per_device(tensor, trial_x, trial_y):
    bond_dim = trial_x.shape[1]
    blocks = tensor.reshape(tensor.shape[0], tensor.shape[1], bond_dim, bond_dim)
    x_pair = x_factors(blocks, bond_dim)
    x_pair = summed_x(x_pair)
    y_pair = y_factors(blocks, bond_dim)
    y_pair = summed_y(y_pair)
    x_up, x_low = x_pair
    y_up, y_low = y_pair
    x_rows = tensor.shape[0]
    y_rows = tensor.shape[1]
    gram_x = lax.dynamic_slice_in_dim(
        compose(x_up, x_low, bond_dim), lax.axis_index("aa") * x_rows, x_rows, 0
    )
    gram_y = lax.dynamic_slice_in_dim(
        compose(y_up, y_low, bond_dim), lax.axis_index("ba") * y_rows, y_rows, 0
    )
    proj_x = jnp.dot(
        gram_x, trial_x, precision=lax.Precision.HIGHEST, preferred_element_type=jnp.float32
    )
    proj_y = jnp.dot(
        gram_y, trial_y, precision=lax.Precision.HIGHEST, preferred_element_type=jnp.float32
    )
    return (gram_x, proj_x, gram_y, proj_y)


def solution(mesh):
    in_specs = (P("aa", "ba", None), P(), P())
    out_specs = (P("aa", None), P("aa", None), P("ba", None), P("ba", None))
    return jax.shard_map(
        per_device, mesh=mesh, in_specs=in_specs, out_specs=out_specs, check_vma=False
    )
```

profile of v0, /device:TPU:1, one launch (start us, length us, event | category | flops | bytes accessed | tf_op | source)
XLA Modules:
  0.0 731.4 jit_solution(9530736843136767235)
XLA Ops:
  7.2 0.0 copy-start
  7.2 6.5 copy.60
  13.6 3.4 copy.73
  17.1 69.0 %all_to_all.60 = bf16[72,864,24]{0,2,1:T(8,128)(2,1)} all-to-all(bf16[72,864,24]{0,2,1:T(8,128)(2,1)S(1)} %bitcast.118), channel_id=1, replica_groups=mesh['aa'=16,'ba'=8] {'ba'}, dimensions={1} | all-to-all | bytes 5971968 | tf_op jit(solution)/shard_map/all_to_all | solution.py:31
  86.1 4.7 all-to-all-start.2
  90.8 18.7 %copy.86 = bf16[36,72,24,24]{0,3,2,1:T(8,128)(2,1)} copy(bf16[36,72,24,24]{1,2,3,0:T(8,128)(2,1)} %bitcast.108) | data formatting | bytes 5971968 | tf_op jit(solution)/shard_map/reshape | solution.py:17
  109.5 18.8 %reshape.102 = bf16[16,2,46656]{2,1,0:T(2,128)(2,1)} reshape(bf16[1728,24,36]{2,1,0:T(8,128)(2,1)} %bitcast.111) | data formatting | bytes 5971968
  128.3 23.1 %all-to-all-done.2 = bf16[72,864,24]{0,2,1:T(8,128)(2,1)} async-done(((bf16[72,864,24]{0,2,1:T(8,128)(2,1)}), bf16[72,864,24]{0,2,1:T(8,128)(2,1)}, u32[]{:S(2)}, u32[]{:S(2)}) %all-to-all-start.2) | async-done | bytes 2986016 | tf_op jit(solution)/shard_map/all_to_all | solution.py:30
  151.4 9.6 %all-to-all-start.1 = ((bf16[16,2,46656]{2,1,0:T(2,128)(2,1)}), bf16[16,2,46656]{2,1,0:T(2,128)(2,1)}, u32[]{:S(2)}, u32[]{:S(2)}) async-start(bf16[16,2,46656]{2,1,0:T(2,128)(2,1)} %reshape.102), calls=%async_computation.1 | async-start | bytes 5980160 | tf_op jit(solution)/shard_map/all_to_all | solution.py:20
  161.0 0.0 copy-done.1
  161.0 7.8 %copy.83 = bf16[36,72,576]{0,2,1:T(8,128)(2,1)} copy(bf16[36,72,576]{2,1,0:T(8,128)(2,1)S(1)} %copy-done.1) | data formatting | bytes 5971968 | tf_op jit(solution)/shard_map/reshape;reshape | solution.py:16
  168.9 18.8 %reshape.104 = bf16[16,2,46656]{2,1,0:T(2,128)(2,1)} reshape(bf16[1728,24,36]{2,1,0:T(8,128)(2,1)} %bitcast.112) | data formatting | bytes 5971968
  187.6 10.2 %all-to-all-done.1 = bf16[16,2,46656]{2,1,0:T(2,128)(2,1)} async-done(((bf16[16,2,46656]{2,1,0:T(2,128)(2,1)}), bf16[16,2,46656]{2,1,0:T(2,128)(2,1)}, u32[]{:S(2)}, u32[]{:S(2)}) %all-to-all-start.1) | async-done | bytes 2986016 | tf_op jit(solution)/shard_map/all_to_all | solution.py:20
  197.8 4.4 all-to-all-start
  202.2 0.5 all-reduce.3.cloned.1.call-start
  202.7 7.3 copy.75
  210.0 2.6 copy.76
  212.6 4.1 bitcast_multiply_fusion.2
  216.7 5.9 reshape.91
  222.6 7.3 copy.69
  229.8 2.6 copy.70
  232.5 4.1 bitcast_multiply_fusion.3
  236.5 5.8 reshape.88
  242.4 21.3 %reshape.103 = bf16[1728,24,36]{2,1,0:T(8,128)(2,1)} reshape(bf16[16,2,46656]{2,1,0:T(2,128)(2,1)} %all-to-all-done.1) | data formatting | bytes 5971968
  263.7 12.6 %copy.64 = bf16[16,36,108,24]{2,3,1,0:T(8,128)(2,1)} copy(bf16[16,36,108,24]{1,3,2,0:T(8,128)(2,1)} %bitcast.109) | data formatting | bytes 5971968 | tf_op jit(solution)/shard_map/all_to_all | solution.py:20
  276.3 2.6 copy.65
  278.9 4.2 bitcast_multiply_fusion.4
  283.1 5.8 reshape.85
  288.9 0.0 all-to-all-done
  288.9 21.1 %reshape.105 = bf16[1728,24,36]{2,1,0:T(8,128)(2,1)} reshape(bf16[16,2,46656]{2,1,0:T(2,128)(2,1)S(1)} %all-to-all-done) | data formatting | bytes 5971968
  310.1 12.5 %copy.56 = bf16[16,36,108,24]{2,3,1,0:T(8,128)(2,1)} copy(bf16[16,36,108,24]{1,3,2,0:T(8,128)(2,1)} %bitcast.110) | data formatting | bytes 5971968 | tf_op jit(solution)/shard_map/all_to_all | solution.py:19
  322.6 2.6 copy.57
  325.2 2.9 bitcast_multiply_fusion.5
  328.2 4.5 reshape.81
  332.7 0.0 all-reduce.3.cloned.1.call-update
  332.8 236.9 %all-reduce.3.cloned.1.call-done = (f32[24,24,24,24]{3,1,2,0:T(8,128)}, f32[24,24,24,24]{3,1,2,0:T(8,128)}, f32[24,24,24,24]{3,1,2,0:T(8,128)}, f32[24,24,24,24]{3,1,2,0:T(8,128)}) async-done(((f32[24,24,24,24]{3,1,2,0:T(8,128)}, f32[24,24,24,24]{3,1,2,0:T(8,128)}, f32[24,24,24,24]{3,1,2,0:T(8,128)}, f32[24,24,24,24]{3,1,2,0:T(8,128)}), (f32[24,24,24,24]{3,1,2,0:T(8,128)}, f32[24,24,24,24]{3,1,2,0:T(8,128)}, ...) | async-done | bytes 5308432 | tf_op jit(solution)/shard_map/psum | solution.py:37
  569.7 71.5 %fusion.4 = f32[24,24,24,24]{3,2,1,0:T(8,128)} fusion(f32[24,24,24,24]{3,1,2,0:T(8,128)} %get-tuple-element.6, f32[24,24,24,24]{3,1,2,0:T(8,128)} %get-tuple-element.7), kind=kOutput, calls=%fused_computation.5 | convolution fusion | flops 2293567488 | bytes 3981312 | tf_op jit(solution)/shard_map/dot_general | solution.py:56
  641.2 4.7 mul.46
  645.9 71.6 %fusion.6 = f32[24,24,24,24]{3,2,1,0:T(8,128)} fusion(f32[24,24,24,24]{3,1,2,0:T(8,128)} %get-tuple-element.4, f32[24,24,24,24]{3,1,2,0:T(8,128)} %get-tuple-element.5), kind=kOutput, calls=%fused_computation.8 | convolution fusion | flops 2293567488 | bytes 3981312 | tf_op jit(solution)/shard_map/dot_general | solution.py:56
  717.6 4.7 mul.40
  722.3 0.0 copy-done
  722.3 0.0 copy-start.2
  722.3 0.9 fusion.33
  723.2 0.0 copy-done.4
  723.2 0.0 copy-start.3
  723.2 0.8 fusion.32
  724.1 0.0 copy-done.2
  724.1 0.0 copy-done.3
  (4 shorter events, 0.0 us)
Async XLA Ops:
  7.2 715.1 %copy-start = (f32[576,24]{0,1:T(8,128)S(1)}, f32[576,24]{0,1:T(8,128)}, u32[]{:S(2)}) copy-start(f32[576,24]{0,1:T(8,128)} %param.5) | copy-start | bytes 165892
  86.1 65.3 %all-to-all-start.2 = ((bf16[72,864,24]{0,2,1:T(8,128)(2,1)}), bf16[72,864,24]{0,2,1:T(8,128)(2,1)}, u32[]{:S(2)}, u32[]{:S(2)}) async-start(bf16[72,864,24]{0,2,1:T(8,128)(2,1)} %bitcast.107), calls=%async_computation.2 | async-start | bytes 10616832 | tf_op jit(solution)/shard_map/all_to_all | solution.py:30
  128.3 32.7 %copy-start.1 = (bf16[36,72,576]{2,1,0:T(8,128)(2,1)S(1)}, bf16[36,72,576]{2,1,0:T(8,128)(2,1)}, u32[]{:S(2)}) copy-start(bf16[36,72,576]{2,1,0:T(8,128)(2,1)} %param.3) | copy-start | bytes 8957956
  151.4 46.4 %all-to-all-start.1 = ((bf16[16,2,46656]{2,1,0:T(2,128)(2,1)}), bf16[16,2,46656]{2,1,0:T(2,128)(2,1)}, u32[]{:S(2)}, u32[]{:S(2)}) async-start(bf16[16,2,46656]{2,1,0:T(2,128)(2,1)} %reshape.102), calls=%async_computation.1 | async-start | bytes 5980160 | tf_op jit(solution)/shard_map/all_to_all | solution.py:20
  197.8 91.1 %all-to-all-start = ((bf16[16,2,46656]{2,1,0:T(2,128)(2,1)}), bf16[16,2,46656]{2,1,0:T(2,128)(2,1)S(1)}, u32[]{:S(2)}, u32[]{:S(2)}) async-start(bf16[16,2,46656]{2,1,0:T(2,128)(2,1)} %reshape.104), calls=%async_computation | async-start | bytes 5980160 | tf_op jit(solution)/shard_map/all_to_all | solution.py:19
  202.2 367.5 %all-reduce.3.cloned.1.call-start = ((), (), s32[]{:S(2)}) async-start(), calls=%async_computation.4 | async-start | bytes 56623104 | tf_op jit(solution)/shard_map/psum | solution.py:37
  717.6 5.7 copy-start.4
  722.3 1.8 copy-start.2
  723.2 0.8 copy-start.3
Sparse Core Ops, SparseCore 0:
  332.9 236.7 all-reduce.2
where the time goes:
time: 738 us; the launch traced here: 731 us
  waiting for transfers between devices  270 us (37%)
  local copies, waits for them, and re-layouts  198 us (27%)
  matrix products  160 us (22%)
  blocking collectives  69 us (9%)
  starting transfers between devices  19.2 us (3%)
  between operations  14.6 us (2%)
    psum x1, waiting for transfers between devices, summed_x(): return lax.psum((factors[0], factors[1]), ('aa', 'ba'))  237 us
    dot_general x2, matrix products, compose(): jnp.dot(up_matrix, low_matrix.T, precision=lax.Precision.HIGHEST, preferr...  143 us
    unnamed x15, local copies, waits for them, and re-layouts  86.5 us
    all_to_all x1, blocking collectives, y_factors(): lax.all_to_all(lower_view, 'ba', split_axis=1, concat_axis=0, tiled=True)  69 us
    all_to_all x1, waiting for transfers between devices, y_factors(): lax.all_to_all(upper_view, 'ba', split_axis=1, concat_axis=0, tiled=True)  23.1 us
    reshape x1, local copies, waits for them, and re-layouts, x_factors(): jnp.swapaxes(blocks, 2, 3).reshape(x_height, y_width * bond_dim, bond_dim)  18.7 us
    dot_general x4, matrix products, leg_factor(): jnp.einsum('aprk,bprl->akbl', shaped, shaped, preferred_element_type=jnp....  15.2 us
  transfers between devices with their start and end apart: 4, of which 3 were waited for; matrix products, arithmetic and copies ran while one was open for 21% of the time, Pallas kernels for 0%

commit v1 on v0

v1 whole, which is shorter than its diff:
```python
import functools

import jax
import jax.numpy as jnp
import numpy as np
from jax import lax
from jax.experimental import pallas as pl
from jax.experimental.pallas import tpu as pltpu
from jax.sharding import PartitionSpec as P

CHI = 24
PAIR = 576
GROUPS = 8
MSG = 32
STACK = GROUPS * MSG
HIGHEST = lax.Precision.HIGHEST
MESH = pl.DeviceIdType.MESH
NT = (((1,), (1,)), ((), ()))


def send_rows():
    out = np.zeros((3, STACK, 72), np.float32)
    for jd in range(8):
        for xs in range(3):
            for y in range(3):
                for ys in range(3):
                    out[xs, jd * MSG + xs * 9 + y * 3 + ys, y * 24 + jd * 3 + ys] = 1
    return out


def y_rows():
    out = np.zeros((240, 256), np.float32)
    for xg in range(8):
        for xs in range(3):
            for y in range(3):
                for ys in range(3):
                    out[y * 80 + xg * 9 + xs * 3 + ys, xg * 32 + xs * 9 + y * 3 + ys] = 1
    return out


def bond_swap():
    out = np.zeros((PAIR, PAIR), np.float32)
    for a in range(CHI):
        for b in range(CHI):
            out[b * CHI + a, a * CHI + b] = 1
    return out


def enter(others_count, signal_all):
    barrier = pltpu.get_barrier_semaphore()
    signal_all(barrier)
    pl.semaphore_wait(barrier, others_count)


def place():
    aa = lax.axis_index("aa")
    ba = lax.axis_index("ba")
    return aa // 2, aa % 2, ba


def greet_core_group(i, c, j):
    def signal_all(barrier):
        def one(n, carry):
            di = n // 8
            dj = n % 8
            same = jnp.logical_and(di == i, dj == j)
            core = jnp.where(same, 1 - c, c)
            pl.semaphore_signal(
                barrier, inc=1, device_id=(2 * di + core, dj), device_id_type=MESH
            )
            return carry

        lax.fori_loop(0, 64, one, 0)

    enter(64, signal_all)


def gram_kernel(
    t_ref, ps_ref, py_ref, eye_ref, swap_ref, q_ref,
    snd, got, zbuf, m_up, m_low, send_sem, recv_sem, fsend_sem, frecv_sem,
):
    i, c, j = place()
    greet_core_group(i, c, j)

    def gather_unit(u, carry):
        rows = jnp.zeros((STACK, PAIR), jnp.float32)
        for xs in range(3):
            rows += jnp.dot(ps_ref[xs], t_ref[3 * u + xs], preferred_element_type=jnp.float32)
        snd[u] = rows.astype(jnp.bfloat16).reshape(GROUPS, MSG, PAIR)
        return carry

    lax.fori_loop(0, 12, gather_unit, 0)

    def send_unit(u, idest):
        x = 3 * i + (12 * c + u) // 8

        def one(s, carry):
            jd = (j + s) % 8
            same = jnp.logical_and(idest == i, jd == j)

            @pl.when(jnp.logical_not(same))
            def _():
                pltpu.make_async_remote_copy(
                    src_ref=snd.at[u, jd],
                    dst_ref=got.at[x, j],
                    send_sem=send_sem.at[u],
                    recv_sem=recv_sem.at[x],
                    device_id=(2 * idest + c, jd),
                    device_id_type=MESH,
                ).start()

            @pl.when(same)
            def _():
                got[x, j] = snd[u, jd]

            return carry

        lax.fori_loop(0, 8, one, 0)

    def send_to(s, carry):
        idest = (i + s) % 8
        first = (idest + 4 * c) % 8
        send_unit(first, idest)

        @pl.when(first < 4)
        def _():
            send_unit(first + 8, idest)

        return carry

    lax.fori_loop(0, 8, send_to, 0)

    sibling = (2 * i + (1 - c), j)
    direct_one = (i < 4) == (c == 0)

    def forward(x):
        return pltpu.make_async_remote_copy(
            src_ref=got.at[x],
            dst_ref=got.at[x],
            send_sem=fsend_sem.at[x],
            recv_sem=frecv_sem.at[x],
            device_id=sibling,
            device_id_type=MESH,
        )

    def take_direct(x, own):
        @pl.when(own)
        def _():
            pltpu.make_async_copy(
                got.at[x, pl.ds(0, 7)], got.at[x, pl.ds(0, 7)], recv_sem.at[x]
            ).wait()

        @pl.when(jnp.logical_not(own))
        def _():
            pltpu.make_async_copy(got.at[x], got.at[x], recv_sem.at[x]).wait()

        forward(x).start()

    def receive(s, carry):
        src = (i + 8 - s) % 8
        own = src == i
        take_direct(3 * src + 2 * c, own)

        @pl.when(direct_one)
        def _():
            take_direct(3 * src + 1, own)

        return carry

    lax.fori_loop(0, 8, receive, 0)

    def receive_forwarded(src, carry):
        forward(3 * src + 2 * (1 - c)).wait_recv()
        forward(3 * src + 2 * c).wait_send()

        @pl.when(direct_one)
        def _():
            forward(3 * src + 1).wait_send()

        @pl.when(jnp.logical_not(direct_one))
        def _():
            forward(3 * src + 1).wait_recv()

        return carry

    lax.fori_loop(0, 8, receive_forwarded, 0)

    def drain(u, carry):
        idest = (12 * c + u) % 8

        @pl.when(idest == i)
        def _():
            pltpu.make_async_copy(
                snd.at[u, pl.ds(0, 7)], snd.at[u, pl.ds(0, 7)], send_sem.at[u]
            ).wait()

        @pl.when(idest != i)
        def _():
            pltpu.make_async_copy(snd.at[u], snd.at[u], send_sem.at[u]).wait()

        return carry

    lax.fori_loop(0, 12, drain, 0)

    @pl.when(c == 1)
    def _():
        def per_group(jd, carry):
            for g in range(3):
                block = got[pl.ds(8 * g, 8), jd].reshape(256, PAIR)
                rows = jnp.dot(py_ref[...], block, preferred_element_type=jnp.float32)
                rows = rows.astype(jnp.bfloat16)
                for y in range(3):
                    zbuf[3 * jd + y, pl.ds(80 * g, 80)] = rows[80 * y : 80 * y + 80]
            for y in range(3):
                zbuf[3 * jd + y, pl.ds(240, 16)] = jnp.zeros((16, PAIR), jnp.bfloat16)
            return carry

        lax.fori_loop(0, 8, per_group, 0)

    @pl.when(c == 0)
    def _():
        def per_x(x, carry):
            zbuf[x] = got[x].reshape(STACK, PAIR)
            return carry

        lax.fori_loop(0, 24, per_x, 0)

    def turn(p, carry):
        for perm, m in ((eye_ref, m_up), (swap_ref, m_low)):
            one = lax.dot_general(perm[...], zbuf[2 * p], NT, preferred_element_type=jnp.float32)
            two = lax.dot_general(perm[...], zbuf[2 * p + 1], NT, preferred_element_type=jnp.float32)
            for z in range(24):
                rows = jnp.concatenate([one[24 * z : 24 * z + 24], two[24 * z : 24 * z + 24]], 0)
                m[pl.ds(pl.multiple_of(48 * p, 16), 48), 256 * z : 256 * z + 256] = rows.astype(
                    jnp.bfloat16
                )
        return carry

    lax.fori_loop(0, 12, turn, 0)

    for which, m in enumerate((m_up, m_low)):
        for col, width in ((0, 256), (256, 256), (512, 64)):
            def step(kk, total):
                ks = pl.ds(pl.multiple_of(kk * 1024, 1024), 1024)
                return total + lax.dot_general(
                    m[:, ks], m[col : col + width, ks], NT, preferred_element_type=jnp.float32
                )

            total = lax.fori_loop(0, 6, step, jnp.zeros((PAIR, width), jnp.float32))
            q_ref[pl.ds(24 * which, 24), :, col : col + width] = total.reshape(24, 24, width)


def relayout(block, st_ref, mask_ref):
    mask = mask_ref[...]
    spread = (block[:, None, :] * mask[None, :, :]).reshape(PAIR, PAIR)
    high = spread.astype(jnp.bfloat16)
    rest = spread - high.astype(jnp.float32)
    mid = rest.astype(jnp.bfloat16)
    low = (rest - mid.astype(jnp.float32)).astype(jnp.bfloat16)
    st = st_ref[...]
    tiled = (
        jnp.dot(high, st, preferred_element_type=jnp.float32)
        + jnp.dot(mid, st, preferred_element_type=jnp.float32)
        + jnp.dot(low, st, preferred_element_type=jnp.float32)
    )
    return jnp.sum(tiled.reshape(CHI, CHI, PAIR) * mask[:, None, :], axis=0)


def compose_kernel(
    q_ref, st_ref, mask_ref, ox_ref, oy_ref,
    parts, mine, ups, lows, outs, send_sem, recv_sem, out_sem, up_sem, low_sem, xsend_sem, xrecv_sem,
):
    i, c, j = place()
    chip = 8 * i + j
    greet_core_group(i, c, j)
    scale = 1.0 / CHI**3
    unit = chip - 16 * c
    owner = jnp.logical_and(unit >= 0, unit < 48)

    def send(s, carry):
        n = (chip + s) % 64
        q = n - 16 * c

        @pl.when(jnp.logical_and(q >= 0, q < 48))
        def _():
            @pl.when(n != chip)
            def _():
                pltpu.make_async_remote_copy(
                    src_ref=q_ref.at[q],
                    dst_ref=parts.at[chip],
                    send_sem=send_sem,
                    recv_sem=recv_sem,
                    device_id=(2 * (n // 8) + c, n % 8),
                    device_id_type=MESH,
                ).start()

            @pl.when(n == chip)
            def _():
                parts[chip] = q_ref[q]

        return carry

    lax.fori_loop(0, 64, send, 0)

    block_index = jnp.where(c == 0, i, j)

    @pl.when(owner)
    def _():
        pltpu.make_async_copy(parts.at[pl.ds(0, 63)], parts.at[pl.ds(0, 63)], recv_sem).wait()

        def add(n, total):
            return total + parts[n]

        total = lax.fori_loop(0, 64, add, jnp.zeros((CHI, PAIR), jnp.float32))
        mine[...] = relayout(total * scale, st_ref, mask_ref)

    is_up = jnp.logical_and(owner, unit < 24)
    is_low = jnp.logical_and(owner, unit >= 24)

    @pl.when(is_up)
    def _():
        def one(s, carry):
            other = jnp.where(c == 0, (j + s) % 8, (i + s) % 8)
            di = jnp.where(c == 0, unit // 3, other)
            dj = jnp.where(c == 0, other, unit // 3)
            same = jnp.logical_and(di == i, dj == j)

            @pl.when(jnp.logical_not(same))
            def _():
                pltpu.make_async_remote_copy(
                    src_ref=mine,
                    dst_ref=ups.at[unit % 3],
                    send_sem=out_sem,
                    recv_sem=up_sem,
                    device_id=(2 * di + c, dj),
                    device_id_type=MESH,
                ).start()

            @pl.when(same)
            def _():
                ups[unit % 3] = mine[...]

            return carry

        lax.fori_loop(0, 8, one, 0)

    @pl.when(is_low)
    def _():
        def one(s, carry):
            n = (chip + s) % 64
            pltpu.make_async_remote_copy(
                src_ref=mine,
                dst_ref=lows.at[unit - 24],
                send_sem=out_sem,
                recv_sem=low_sem,
                device_id=(2 * (n // 8) + c, n % 8),
                device_id_type=MESH,
            ).start()
            return carry

        lax.fori_loop(1, 64, one, 0)
        lows[unit - 24] = mine[...]

    own_up = jnp.logical_and(is_up, unit // 3 == block_index)

    def take(ref, count, sem):
        pltpu.make_async_copy(ref.at[pl.ds(0, count)], ref.at[pl.ds(0, count)], sem).wait()

    @pl.when(own_up)
    def _():
        take(ups, 2, up_sem)

    @pl.when(jnp.logical_not(own_up))
    def _():
        take(ups, 3, up_sem)

    @pl.when(is_low)
    def _():
        take(lows, 23, low_sem)

    @pl.when(jnp.logical_not(is_low))
    def _():
        take(lows, 24, low_sem)

    outs[c] = lax.dot_general(
        ups[...].reshape(72, PAIR), lows[...].reshape(PAIR, PAIR), NT,
        precision=HIGHEST, preferred_element_type=jnp.float32,
    ) * scale
    swap = pltpu.make_async_remote_copy(
        src_ref=outs.at[c],
        dst_ref=outs.at[c],
        send_sem=xsend_sem,
        recv_sem=xrecv_sem,
        device_id=(2 * i + (1 - c), j),
        device_id_type=MESH,
    )
    swap.start()

    @pl.when(owner)
    def _():
        take(q_ref, 47, send_sem)

    @pl.when(jnp.logical_not(owner))
    def _():
        take(q_ref, 48, send_sem)

    @pl.when(is_low)
    def _():
        take(parts, 63, out_sem)

    @pl.when(own_up)
    def _():
        take(parts, 7, out_sem)

    @pl.when(jnp.logical_and(is_up, jnp.logical_not(own_up)))
    def _():
        take(parts, 8, out_sem)

    swap.wait()
    ox_ref[...] = outs[0]
    oy_ref[...] = outs[1]


def per_device(tensor, trial_x, trial_y):
    vmem = pl.BlockSpec(memory_space=pltpu.VMEM)
    dma = pltpu.SemaphoreType.DMA
    factors = pl.pallas_call(
        gram_kernel,
        out_shape=jax.ShapeDtypeStruct((48, CHI, PAIR), jnp.float32),
        in_specs=[vmem] * 5,
        out_specs=vmem,
        scratch_shapes=[
            pltpu.VMEM((12, GROUPS, MSG, PAIR), jnp.bfloat16),
            pltpu.VMEM((24, GROUPS, MSG, PAIR), jnp.bfloat16),
            pltpu.VMEM((24, STACK, PAIR), jnp.bfloat16),
            pltpu.VMEM((PAIR, 24 * 256), jnp.bfloat16),
            pltpu.VMEM((PAIR, 24 * 256), jnp.bfloat16),
            dma((12,)),
            dma((24,)),
            dma((24,)),
            dma((24,)),
        ],
        compiler_params=pltpu.CompilerParams(
            collective_id=0, has_side_effects=True, vmem_limit_bytes=60 * 2**20
        ),
        name="redistribute_and_gram",
    )(
        tensor,
        jnp.asarray(send_rows(), jnp.bfloat16),
        jnp.asarray(y_rows(), jnp.bfloat16),
        jnp.asarray(np.eye(PAIR), jnp.bfloat16),
        jnp.asarray(bond_swap(), jnp.bfloat16),
    )
    index = np.arange(PAIR)
    tile = (index[:, None] % CHI == index[None, :] % CHI).astype(np.float32)
    mask = (np.arange(CHI)[:, None] == index[None, :] // CHI).astype(np.float32)
    out_x, out_y = pl.pallas_call(
        compose_kernel,
        out_shape=[jax.ShapeDtypeStruct((72, PAIR), jnp.float32)] * 2,
        in_specs=[vmem] * 3,
        out_specs=[vmem] * 2,
        scratch_shapes=[
            pltpu.VMEM((64, CHI, PAIR), jnp.float32),
            pltpu.VMEM((CHI, PAIR), jnp.float32),
            pltpu.VMEM((3, CHI, PAIR), jnp.float32),
            pltpu.VMEM((24, CHI, PAIR), jnp.float32),
            pltpu.VMEM((2, 72, PAIR), jnp.float32),
            dma, dma, dma, dma, dma, dma, dma,
        ],
        compiler_params=pltpu.CompilerParams(
            collective_id=1, has_side_effects=True, vmem_limit_bytes=60 * 2**20
        ),
        name="reduce_and_compose",
    )(factors, jnp.asarray(tile, jnp.bfloat16), jnp.asarray(mask, jnp.float32))

    def merged(out):
        return out.reshape(3, CHI, CHI, CHI).transpose(0, 2, 1, 3).reshape(72, PAIR)

    core = lax.axis_index("aa") % 2
    gram_x = lax.dynamic_slice_in_dim(merged(out_x), core * 36, 36, 0)
    gram_y = merged(out_y)
    proj_x = jnp.dot(gram_x, trial_x, precision=HIGHEST, preferred_element_type=jnp.float32)
    proj_y = jnp.dot(gram_y, trial_y, precision=HIGHEST, preferred_element_type=jnp.float32)
    return (gram_x, proj_x, gram_y, proj_y)


def solution(mesh):
    in_specs = (P("aa", "ba", None), P(), P())
    out_specs = (P("aa", None), P("aa", None), P("ba", None), P("ba", None))
    return jax.shard_map(
        per_device, mesh=mesh, in_specs=in_specs, out_specs=out_specs, check_vma=False
    )
```

time: 738 us -> 253 us (0.34)
  the two profiles are of different devices: /device:TPU:1 before, /device:TPU:67 now
where the time goes in v1:
time: 253 us
  Pallas kernels  248 us (98%)
  local copies, waits for them, and re-layouts  2.57 us (1%)
    pallas_call x1, Pallas kernels, per_device(): pl.pallas_call(compose_kernel, out_shape=[jax.ShapeDtypeStruct((72, PAIR)...  130 us
    pallas_call x1, Pallas kernels, per_device(): pl.pallas_call(gram_kernel, out_shape=jax.ShapeDtypeStruct((48, CHI, PAIR...  118 us

profile of v1, /device:TPU:67, one launch (start us, length us, event | category | flops | bytes accessed | tf_op | source)
XLA Modules:
  0.0 253.3 jit_solution(4058479921202287091)
XLA Ops:
  0.6 0.0 copy-start
  0.6 118.2 %redistribute_and_gram.1.q_ref = f32[48,24,576]{2,1,0:T(8,128)} custom-call(bf16[36,72,576]{2,1,0:T(8,128)(2,1)} %t_ref.1, bf16[3,256,72]{2,1,0:T(8,128)(2,1)} %constant.36.clone.ps_ref, bf16[240,256]{1,0:T(8,128)(2,1)} %constant.37.clone.py_ref, bf16[576,576]{1,0:T(8,128)(2,1)} %constant.38.clone.eye_ref, bf16[576,576]{1,0:T(8,128)(2,1)} %constant.39.clone.swap_ref), custom_call_target="tpu_custom_call" | custom-call | tf_op jit(solution)/shard_map/redistribute_and_gram/pallas_call | solution.py:427
  118.9 0.0 copy-start.4
  118.9 130.0 %reduce_and_compose.1 = (f32[72,576]{1,0:T(8,128)}, f32[72,576]{1,0:T(8,128)}) custom-call(f32[48,24,576]{2,1,0:T(8,128)} %redistribute_and_gram.1.q_ref, bf16[576,576]{1,0:T(8,128)(2,1)} %constant.40.clone.st_ref, f32[24,576]{1,0:T(8,128)} %constant.41.clone.mask_ref), custom_call_target="tpu_custom_call" | custom-call | tf_op jit(solution)/shard_map/reduce_and_compose/pallas_call | solution.py:457
  248.9 0.0 copy-start.3
  248.9 1.3 reshape.20
  250.2 0.2 copy.13
  250.4 0.3 reshape.21
  250.7 0.0 copy-done.4
  250.7 0.0 copy-start.2
  250.7 0.8 fusion
  251.6 0.0 copy-done.3
  251.6 0.3 reshape.22
  251.9 0.2 copy.14
  252.1 0.3 reshape.23
  252.4 0.0 copy-done
  252.4 0.0 copy-start.1
  252.4 0.9 fusion.1
  253.3 0.0 copy-done.2
  253.3 0.0 copy-done.1
  (1 shorter events, 0.0 us)
Async XLA Ops:
  0.6 251.8 %copy-start = (f32[576,24]{0,1:T(8,128)S(1)}, f32[576,24]{0,1:T(8,128)}, u32[]{:S(2)}) copy-start(f32[576,24]{0,1:T(8,128)} %param.11) | copy-start | bytes 165892
  118.9 131.8 %copy-start.4 = (f32[576,24]{0,1:T(8,128)S(1)}, f32[576,24]{0,1:T(8,128)}, u32[]{:S(2)}) copy-start(f32[576,24]{0,1:T(8,128)} %param.10) | copy-start | bytes 165892
  248.9 2.7 %copy-start.3 = (f32[72,576]{1,0:T(8,128)S(1)}, f32[72,576]{1,0:T(8,128)}, u32[]{:S(2)}) copy-start(f32[72,576]{1,0:T(8,128)} %get-tuple-element.7) | copy-start | bytes 497668
  250.7 2.6 %copy-start.2 = (f32[36,576]{1,0:T(8,128)}, f32[36,576]{1,0:T(8,128)S(1)}, u32[]{:S(2)}) copy-start(f32[36,576]{1,0:T(8,128)S(1)} %constant_dynamic-slice_fusion) | copy-start | bytes 248836
  252.4 0.9 copy-start.1

commit v2 on v1

--- a/solution.py
+++ b/solution.py
@@ -18,6 +18,19 @@
 NT = (((1,), (1,)), ((), ()))
 
 
+def greet_all(i, c, j):
+    def signal_all(barrier):
+        def one(n, carry):
+            pl.semaphore_signal(
+                barrier, inc=1, device_id=(n // 8, n % 8), device_id_type=MESH
+            )
+            return carry
+
+        lax.fori_loop(0, 128, one, 0)
+
+    enter(128, signal_all)
+
+
 def send_rows():
     out = np.zeros((3, STACK, 72), np.float32)
     for jd in range(8):
@@ -56,6 +69,22 @@
     aa = lax.axis_index("aa")
     ba = lax.axis_index("ba")
     return aa // 2, aa % 2, ba
+
+
+def coordinates():
+    aa = lax.axis_index("aa")
+    ba = lax.axis_index("ba")
+    return aa // 4, (aa // 2) % 2 + 2 * (ba % 2), ba // 2
+
+
+def chip_at(z, x, y):
+    return 2 * z + x % 2, 2 * y + x // 2
+
+
+def shifted(k):
+    z, x, y = coordinates()
+    first, second, third = k % 4, (k // 4) % 4, k // 16
+    return chip_at((z + first) % 4, (x + second + first) % 4, (y + third + 2 * second + first) % 4)
 
 
 def greet_core_group(i, c, j):
@@ -91,44 +120,37 @@
 
     lax.fori_loop(0, 12, gather_unit, 0)
 
-    def send_unit(u, idest):
+    def send_unit(u, idest, jdest):
         x = 3 * i + (12 * c + u) // 8
-
-        def one(s, carry):
-            jd = (j + s) % 8
-            same = jnp.logical_and(idest == i, jd == j)
-
-            @pl.when(jnp.logical_not(same))
-            def _():
-                pltpu.make_async_remote_copy(
-                    src_ref=snd.at[u, jd],
-                    dst_ref=got.at[x, j],
-                    send_sem=send_sem.at[u],
-                    recv_sem=recv_sem.at[x],
-                    device_id=(2 * idest + c, jd),
-                    device_id_type=MESH,
-                ).start()
-
-            @pl.when(same)
-            def _():
-                got[x, j] = snd[u, jd]
-
-            return carry
-
-        lax.fori_loop(0, 8, one, 0)
-
-    def send_to(s, carry):
-        idest = (i + s) % 8
+        same = jnp.logical_and(idest == i, jdest == j)
+
+        @pl.when(jnp.logical_not(same))
+        def _():
+            pltpu.make_async_remote_copy(
+                src_ref=snd.at[u, jdest],
+                dst_ref=got.at[x, j],
+                send_sem=send_sem.at[u],
+                recv_sem=recv_sem.at[x],
+                device_id=(2 * idest + c, jdest),
+                device_id_type=MESH,
+            ).start()
+
+        @pl.when(same)
+        def _():
+            got[x, j] = snd[u, jdest]
+
+    def send_to(k, carry):
+        idest, jdest = shifted(k)
         first = (idest + 4 * c) % 8
-        send_unit(first, idest)
+        send_unit(first, idest, jdest)
 
         @pl.when(first < 4)
         def _():
-            send_unit(first + 8, idest)
+            send_unit(first + 8, idest, jdest)
 
         return carry
 
-    lax.fori_loop(0, 8, send_to, 0)
+    lax.fori_loop(0, 64, send_to, 0)
 
     sibling = (2 * i + (1 - c), j)
     direct_one = (i < 4) == (c == 0)
@@ -268,157 +290,215 @@
 
 def compose_kernel(
     q_ref, st_ref, mask_ref, ox_ref, oy_ref,
-    parts, mine, ups, lows, outs, send_sem, recv_sem, out_sem, up_sem, low_sem, xsend_sem, xrecv_sem,
+    parts1, parts2, parts3, sums1, sums2, mine, ups, lows, piece,
+    s1_sem, r1_sem, s2_sem, r2_sem, s3_sem, r3_sem, out_sem, up_sem, low_sem, x_sem, rx_sem, ry_sem,
 ):
     i, c, j = place()
-    chip = 8 * i + j
-    greet_core_group(i, c, j)
+    greet_all(i, c, j)
     scale = 1.0 / CHI**3
-    unit = chip - 16 * c
-    owner = jnp.logical_and(unit >= 0, unit < 48)
-
-    def send(s, carry):
-        n = (chip + s) % 64
-        q = n - 16 * c
-
-        @pl.when(jnp.logical_and(q >= 0, q < 48))
-        def _():
-            @pl.when(n != chip)
-            def _():
-                pltpu.make_async_remote_copy(
-                    src_ref=q_ref.at[q],
-                    dst_ref=parts.at[chip],
-                    send_sem=send_sem,
-                    recv_sem=recv_sem,
-                    device_id=(2 * (n // 8) + c, n % 8),
-                    device_id_type=MESH,
-                ).start()
-
-            @pl.when(n == chip)
-            def _():
-                parts[chip] = q_ref[q]
-
-        return carry
-
-    lax.fori_loop(0, 64, send, 0)
-
-    block_index = jnp.where(c == 0, i, j)
+    here = coordinates()
+
+    def moved(axis, to):
+        to_coords = [to if a == axis else here[a] for a in range(3)]
+        di, dj = chip_at(*to_coords)
+        return 2 * di + c, dj
+
+    def axes(part):
+        return part, (part + 1) % 3, (part + 2) % 3
+
+    def others(axis, body):
+        def one(s, carry):
+            body((here[axis] + s) % 4)
+            return carry
+
+        lax.fori_loop(1, 4, one, 0)
+
+    def wait_for(ref, sem):
+        pltpu.make_async_copy(ref, ref, sem).wait()
+
+    for part in range(3):
+        first = axes(part)[0]
+
+        def send(to, part=part, first=first):
+            pltpu.make_async_remote_copy(
+                src_ref=q_ref.at[pl.ds(16 * part + 4 * to, 4)],
+                dst_ref=parts1.at[part, here[first]],
+                send_sem=s1_sem.at[part],
+                recv_sem=r1_sem.at[part],
+                device_id=moved(first, to),
+                device_id_type=MESH,
+            ).start()
+
+        others(first, send)
+        parts1[part, here[first]] = q_ref[pl.ds(16 * part + 4 * here[first], 4)]
+
+    for part in range(3):
+        second = axes(part)[1]
+        wait_for(parts1.at[part, pl.ds(0, 3)], r1_sem.at[part])
+        sums1[part] = (parts1[part, 0] + parts1[part, 1]) + (parts1[part, 2] + parts1[part, 3])
+
+        def send(to, part=part, second=second):
+            pltpu.make_async_remote_copy(
+                src_ref=sums1.at[part, to],
+                dst_ref=parts2.at[part, here[second]],
+                send_sem=s2_sem.at[part],
+                recv_sem=r2_sem.at[part],
+                device_id=moved(second, to),
+                device_id_type=MESH,
+            ).start()
+
+        others(second, send)
+        parts2[part, here[second]] = sums1[part, here[second]]
+
+    owned = (here[0] + here[1] + here[2]) % 4
+    for part in range(3):
+        third = axes(part)[2]
+        wait_for(parts2.at[part, pl.ds(0, 3)], r2_sem.at[part])
+        sums2[part] = (parts2[part, 0] + parts2[part, 1]) + (parts2[part, 2] + parts2[part, 3])
+
+        @pl.when(owned == part)
+        def _(part=part, third=third):
+            parts3[here[third]] = sums2[part]
+
+        @pl.when(owned != part)
+        def _(part=part, third=third):
+            to = (part + 8 - here[axes(part)[0]] - here[axes(part)[1]]) % 4
+            pltpu.make_async_remote_copy(
+                src_ref=sums2.at[part],
+                dst_ref=parts3.at[here[third]],
+                send_sem=s3_sem.at[part],
+                recv_sem=r3_sem,
+                device_id=moved(third, to),
+                device_id_type=MESH,
+            ).start()
+
+    unit = 16 * owned + 4 * jnp.where(
+        owned == 0, here[0], jnp.where(owned == 1, here[1], here[2])
+    ) + jnp.where(owned == 0, here[1], jnp.where(owned == 1, here[2], here[0]))
+    owner = owned < 3
 
     @pl.when(owner)
     def _():
-        pltpu.make_async_copy(parts.at[pl.ds(0, 63)], parts.at[pl.ds(0, 63)], recv_sem).wait()
-
-        def add(n, total):
-            return total + parts[n]
-
-        total = lax.fori_loop(0, 64, add, jnp.zeros((CHI, PAIR), jnp.float32))
+        wait_for(parts3.at[pl.ds(0, 3)], r3_sem)
+        total = (parts3[0] + parts3[1]) + (parts3[2] + parts3[3])
         mine[...] = relayout(total * scale, st_ref, mask_ref)
 
     is_up = jnp.logical_and(owner, unit < 24)
     is_low = jnp.logical_and(owner, unit >= 24)
-
-    @pl.when(is_up)
-    def _():
+    local = jnp.where(is_up, unit, unit - 24)
+    by_i = is_up == (c == 0)
+    block = local // 3
+    keeps = jnp.logical_and(owner, jnp.where(by_i, i, j) == block)
+
+    def deliver(slots, sem):
         def one(s, carry):
-            other = jnp.where(c == 0, (j + s) % 8, (i + s) % 8)
-            di = jnp.where(c == 0, unit // 3, other)
-            dj = jnp.where(c == 0, other, unit // 3)
+            other = jnp.where(by_i, (j + s) % 8, (i + s) % 8)
+            di = jnp.where(by_i, block, other)
+            dj = jnp.where(by_i, other, block)
             same = jnp.logical_and(di == i, dj == j)
 
             @pl.when(jnp.logical_not(same))
             def _():
                 pltpu.make_async_remote_copy(
                     src_ref=mine,
-                    dst_ref=ups.at[unit % 3],
+                    dst_ref=slots.at[local % 3],
                     send_sem=out_sem,
-                    recv_sem=up_sem,
+                    recv_sem=sem,
                     device_id=(2 * di + c, dj),
                     device_id_type=MESH,
                 ).start()
 
             @pl.when(same)
             def _():
-                ups[unit % 3] = mine[...]
+                slots[local % 3] = mine[...]
 
             return carry
 
         lax.fori_loop(0, 8, one, 0)
 
+    @pl.when(is_up)
+    def _():
+        deliver(ups, up_sem)
+
     @pl.when(is_low)
     def _():
+        deliver(lows, low_sem)
+
+    def take(ref, count, sem):
+        wait_for(ref.at[pl.ds(0, count)], sem)
+
+    def take_rows(slots, kept, sem):
+        @pl.when(kept)
+        def _():
+            take(slots, 2, sem)
+
+        @pl.when(jnp.logical_not(kept))
+        def _():
+            take(slots, 3, sem)
+
+    take_rows(ups, jnp.logical_and(keeps, is_up), up_sem)
+    take_rows(lows, jnp.logical_and(keeps, is_low), low_sem)
+
+    piece[...] = lax.dot_general(
+        ups[...].reshape(72, PAIR), lows[...].reshape(72, PAIR), NT,
+        precision=HIGHEST, preferred_element_type=jnp.float32,
+    ) * scale
+
+    def spread(out_ref, slot, sem):
         def one(s, carry):
-            n = (chip + s) % 64
+            core = (c + s) % 2
+            other = s // 2
+            di = jnp.where(c == 0, i, (i + other) % 8)
+            dj = jnp.where(c == 0, (j + other) % 8, j)
             pltpu.make_async_remote_copy(
-                src_ref=mine,
-                dst_ref=lows.at[unit - 24],
-                send_sem=out_sem,
-                recv_sem=low_sem,
-                device_id=(2 * (n // 8) + c, n % 8),
+                src_ref=piece,
+                dst_ref=out_ref.at[slot],
+                send_sem=x_sem.at[s % 2],
+                recv_sem=sem,
+                device_id=(2 * di + core, dj),
                 device_id_type=MESH,
             ).start()
             return carry
 
-        lax.fori_loop(1, 64, one, 0)
-        lows[unit - 24] = mine[...]
-
-    own_up = jnp.logical_and(is_up, unit // 3 == block_index)
-
-    def take(ref, count, sem):
-        pltpu.make_async_copy(ref.at[pl.ds(0, count)], ref.at[pl.ds(0, count)], sem).wait()
-
-    @pl.when(own_up)
-    def _():
-        take(ups, 2, up_sem)
-
-    @pl.when(jnp.logical_not(own_up))
-    def _():
-        take(ups, 3, up_sem)
-
-    @pl.when(is_low)
-    def _():
-        take(lows, 23, low_sem)
-
-    @pl.when(jnp.logical_not(is_low))
-    def _():
-        take(lows, 24, low_sem)
-
-    outs[c] = lax.dot_general(
-        ups[...].reshape(72, PAIR), lows[...].reshape(PAIR, PAIR), NT,
-        precision=HIGHEST, preferred_element_type=jnp.float32,
-    ) * scale
-    swap = pltpu.make_async_remote_copy(
-        src_ref=outs.at[c],
-        dst_ref=outs.at[c],
-        send_sem=xsend_sem,
-        recv_sem=xrecv_sem,
-        device_id=(2 * i + (1 - c), j),
-        device_id_type=MESH,
-    )
-    swap.start()
-
-    @pl.when(owner)
-    def _():
-        take(q_ref, 47, send_sem)
-
-    @pl.when(jnp.logical_not(owner))
-    def _():
-        take(q_ref, 48, send_sem)
-
-    @pl.when(is_low)
-    def _():
-        take(parts, 63, out_sem)
-
-    @pl.when(own_up)
-    def _():
-        take(parts, 7, out_sem)
-
-    @pl.when(jnp.logical_and(is_up, jnp.logical_not(own_up)))
-    def _():
-        take(parts, 8, out_sem)
-
-    swap.wait()
-    ox_ref[...] = outs[0]
-    oy_ref[...] = outs[1]
+        lax.fori_loop(1, 16, one, 0)
+        out_ref[slot] = piece[...]
+
+    @pl.when(c == 0)
+    def _():
+        spread(ox_ref, j, rx_sem)
+
+    @pl.when(c == 1)
+    def _():
+        spread(oy_ref, i, ry_sem)
+
+    for part in range(3):
+        wait_for(q_ref.at[pl.ds(0, 12)], s1_sem.at[part])
+        wait_for(sums1.at[part, pl.ds(0, 3)], s2_sem.at[part])
+
+        @pl.when(owned != part)
+        def _(part=part):
+            wait_for(sums2.at[part], s3_sem.at[part])
+
+    @pl.when(keeps)
+    def _():
+        take(q_ref, 7, out_sem)
+
+    @pl.when(jnp.logical_and(owner, jnp.logical_not(keeps)))
+    def _():
+        take(q_ref, 8, out_sem)
+
+    take(ox_ref, 7, x_sem.at[0])
+    take(ox_ref, 8, x_sem.at[1])
+
+    @pl.when(c == 0)
+    def _():
+        take(ox_ref, 7, rx_sem)
+        take(oy_ref, 8, ry_sem)
+
+    @pl.when(c == 1)
+    def _():
+        take(ox_ref, 8, rx_sem)
+        take(oy_ref, 7, ry_sem)
 
 
 def per_device(tensor, trial_x, trial_y):
@@ -456,16 +536,21 @@
     mask = (np.arange(CHI)[:, None] == index[None, :] // CHI).astype(np.float32)
     out_x, out_y = pl.pallas_call(
         compose_kernel,
-        out_shape=[jax.ShapeDtypeStruct((72, PAIR), jnp.float32)] * 2,
+        out_shape=[jax.ShapeDtypeStruct((8, 72, 72), jnp.float32)] * 2,
         in_specs=[vmem] * 3,
         out_specs=[vmem] * 2,
         scratch_shapes=[
-            pltpu.VMEM((64, CHI, PAIR), jnp.float32),
+            pltpu.VMEM((3, 4, 4, CHI, PAIR), jnp.float32),
+            pltpu.VMEM((3, 4, CHI, PAIR), jnp.float32),
+            pltpu.VMEM((4, CHI, PAIR), jnp.float32),
+            pltpu.VMEM((3, 4, CHI, PAIR), jnp.float32),
+            pltpu.VMEM((3, CHI, PAIR), jnp.float32),
             pltpu.VMEM((CHI, PAIR), jnp.float32),
             pltpu.VMEM((3, CHI, PAIR), jnp.float32),
-            pltpu.VMEM((24, CHI, PAIR), jnp.float32),
-            pltpu.VMEM((2, 72, PAIR), jnp.float32),
-            dma, dma, dma, dma, dma, dma, dma,
+            pltpu.VMEM((3, CHI, PAIR), jnp.float32),
+            pltpu.VMEM((72, 72), jnp.float32),
+            dma((3,)), dma((3,)), dma((3,)), dma((3,)), dma((3,)),
+            dma, dma, dma, dma, dma((2,)), dma, dma,
         ],
         compiler_params=pltpu.CompilerParams(
             collective_id=1, has_side_effects=True, vmem_limit_bytes=60 * 2**20
@@ -474,7 +559,7 @@
     )(factors, jnp.asarray(tile, jnp.bfloat16), jnp.asarray(mask, jnp.float32))
 
     def merged(out):
-        return out.reshape(3, CHI, CHI, CHI).transpose(0, 2, 1, 3).reshape(72, PAIR)
+        return out.reshape(8, 3, CHI, 3, CHI).transpose(1, 0, 3, 2, 4).reshape(72, PAIR)
 
     core = lax.axis_index("aa") % 2
     gram_x = lax.dynamic_slice_in_dim(merged(out_x), core * 36, 36, 0)

time: 253 us -> 170 us (0.67)
  the two profiles are of different devices: /device:TPU:67 before, /device:TPU:1 now
where the time goes in v2:
time: 170 us; the launch traced here: 169 us
  Pallas kernels  164 us (96%)
  local copies, waits for them, and re-layouts  2.74 us (2%)
  matrix products  1.73 us (1%)
    pallas_call x1, Pallas kernels, per_device(): pl.pallas_call(gram_kernel, out_shape=jax.ShapeDtypeStruct((48, CHI, PAIR...  109 us
    pallas_call x1, Pallas kernels, per_device(): pl.pallas_call(compose_kernel, out_shape=[jax.ShapeDtypeStruct((8, 72, 72...  55 us

profile of v2, /device:TPU:1, one launch (start us, length us, event | category | flops | bytes accessed | tf_op | source)
XLA Modules:
  0.0 169.1 jit_solution(3300413304120832804)
XLA Ops:
  0.6 0.0 copy-start
  0.6 108.8 %redistribute_and_gram.1.q_ref = f32[48,24,576]{2,1,0:T(8,128)} custom-call(bf16[36,72,576]{2,1,0:T(8,128)(2,1)} %t_ref.1, bf16[3,256,72]{2,1,0:T(8,128)(2,1)} %constant.36.clone.ps_ref, bf16[240,256]{1,0:T(8,128)(2,1)} %constant.37.clone.py_ref, bf16[576,576]{1,0:T(8,128)(2,1)} %constant.38.clone.eye_ref, bf16[576,576]{1,0:T(8,128)(2,1)} %constant.39.clone.swap_ref), custom_call_target="tpu_custom_call" | custom-call | tf_op jit(solution)/shard_map/redistribute_and_gram/pallas_call | solution.py:507
  109.5 55.0 %reduce_and_compose.1 = (f32[8,72,72]{2,1,0:T(8,128)}, f32[8,72,72]{2,1,0:T(8,128)}) custom-call(f32[48,24,576]{2,1,0:T(8,128)} %redistribute_and_gram.1.q_ref, bf16[576,576]{1,0:T(8,128)(2,1)} %constant.40.clone.st_ref, f32[24,576]{1,0:T(8,128)} %constant.41.clone.mask_ref), custom_call_target="tpu_custom_call" | custom-call | tf_op jit(solution)/shard_map/reduce_and_compose/pallas_call | solution.py:537
  164.5 0.0 copy-start.4
  164.5 0.0 copy-start.3
  164.5 1.6 reshape.20
  166.1 0.1 copy.15
  166.2 0.3 reshape.21
  166.5 0.0 copy-done.4
  166.5 0.0 copy-start.2
  166.5 0.8 fusion
  167.4 0.0 copy-done.3
  167.4 0.4 reshape.22
  167.8 0.1 copy.16
  167.9 0.3 reshape.23
  168.2 0.0 copy-done
  168.2 0.0 copy-start.1
  168.2 0.9 fusion.1
  169.1 0.0 copy-done.2
  169.1 0.0 copy-done.1
  (1 shorter events, 0.0 us)
Async XLA Ops:
  0.6 167.5 %copy-start = (f32[576,24]{0,1:T(8,128)S(1)}, f32[576,24]{0,1:T(8,128)}, u32[]{:S(2)}) copy-start(f32[576,24]{0,1:T(8,128)} %param.11) | copy-start | bytes 165892
  164.5 2.0 %copy-start.4 = (f32[576,24]{0,1:T(8,128)S(1)}, f32[576,24]{0,1:T(8,128)}, u32[]{:S(2)}) copy-start(f32[576,24]{0,1:T(8,128)} %param.10) | copy-start | bytes 165892
  164.5 2.8 %copy-start.3 = (f32[8,72,72]{2,1,0:T(8,128)S(1)}, f32[8,72,72]{2,1,0:T(8,128)}, u32[]{:S(2)}) copy-start(f32[8,72,72]{2,1,0:T(8,128)} %get-tuple-element.7) | copy-start | bytes 497668
  166.5 2.6 %copy-start.2 = (f32[36,576]{1,0:T(8,128)}, f32[36,576]{1,0:T(8,128)S(1)}, u32[]{:S(2)}) copy-start(f32[36,576]{1,0:T(8,128)S(1)} %constant_dynamic-slice_fusion) | copy-start | bytes 248836
  168.2 0.9 copy-start.1

commit v3 on v2

v3 whole, which is shorter than its diff:
```python
import functools

import jax
import jax.numpy as jnp
import numpy as np
from jax import lax
from jax.experimental import pallas as pl
from jax.experimental.pallas import tpu as pltpu
from jax.sharding import PartitionSpec as P

CHI = 24
PAIR = 576
GROUPS = 8
MSG = 32
STACK = GROUPS * MSG
HIGHEST = lax.Precision.HIGHEST
MESH = pl.DeviceIdType.MESH
NT = (((1,), (1,)), ((), ()))


def send_rows():
    out = np.zeros((STACK, 216), np.float32)
    for jd in range(8):
        for xs in range(3):
            for y in range(3):
                for ys in range(3):
                    h, r = divmod(xs * 9 + y * 3 + ys, 16)
                    out[h * 128 + jd * 16 + r, xs * 72 + y * 24 + jd * 3 + ys] = 1
    return out


def y_rows():
    out = np.zeros((240, 256), np.float32)
    for xg in range(8):
        for xs in range(3):
            for y in range(3):
                for ys in range(3):
                    h, r = divmod(xs * 9 + y * 3 + ys, 16)
                    out[y * 80 + xg * 9 + xs * 3 + ys, h * 128 + xg * 16 + r] = 1
    return out


def place():
    aa = lax.axis_index("aa")
    ba = lax.axis_index("ba")
    return aa // 2, aa % 2, ba


def coordinates():
    aa = lax.axis_index("aa")
    ba = lax.axis_index("ba")
    return aa // 4, (aa // 2) % 2 + 2 * (ba % 2), ba // 2


def chip_at(z, x, y):
    return 2 * z + x % 2, 2 * y + x // 2


def shift_of(k):
    quarter, rest = k // 16, k % 16
    low, high = rest % 4, rest // 4
    dz = 2 * (low % 2) + quarter // 2
    dx = (low + high) % 4
    dy = 2 * ((high + low // 2) % 2) + quarter % 2
    return dz, dx, dy


def partner(k, sign):
    z, x, y = coordinates()
    dz, dx, dy = shift_of(k)
    return chip_at((z + 4 + sign * dz) % 4, (x + 4 + sign * dx) % 4, (y + 4 + sign * dy) % 4)


def wait_for(ref, sem):
    pltpu.make_async_copy(ref, ref, sem).wait()


def take(ref, count, sem):
    wait_for(ref.at[pl.ds(0, count)], sem)


def greet(i, c, j, barrier):
    def one(n, carry):
        di, dj = n // 8, n % 8

        @pl.when(jnp.logical_not(jnp.logical_and(di == i, dj == j)))
        def _():
            pl.semaphore_signal(barrier, inc=1, device_id=(2 * di + c, dj), device_id_type=MESH)

        return carry

    lax.fori_loop(0, 64, one, 0)

    def across(n, carry):
        di = jnp.where(c == 0, n, i)
        dj = jnp.where(c == 0, j, n)
        pl.semaphore_signal(barrier, inc=1, device_id=(2 * di + 1 - c, dj), device_id_type=MESH)
        return carry

    lax.fori_loop(0, 8, across, 0)


def relayout(block, st_ref, mask_ref):
    mask = mask_ref[...]
    spread = (block[:, None, :] * mask[None, :, :]).reshape(PAIR, PAIR)
    high = spread.astype(jnp.bfloat16)
    rest = spread - high.astype(jnp.float32)
    mid = rest.astype(jnp.bfloat16)
    low = (rest - mid.astype(jnp.float32)).astype(jnp.bfloat16)
    st = st_ref[...]
    tiled = (
        jnp.dot(high, st, preferred_element_type=jnp.float32)
        + jnp.dot(mid, st, preferred_element_type=jnp.float32)
        + jnp.dot(low, st, preferred_element_type=jnp.float32)
    )
    return jnp.sum(tiled.reshape(CHI, CHI, PAIR) * mask[:, None, :], axis=0)


def fused_kernel(
    t_ref, ps_ref, py_ref, eye_ref, st_ref, mask_ref, ox_ref, oy_ref,
    snd, got, zbuf, turned, m_up, m_low, q_ref,
    send_sem, recv_sem, fsend_sem, frecv_sem,
    parts1, parts2, parts3, sums1, sums2, mine, ups, lows, piece,
    s1_sem, r1_sem, s2_sem, r2_sem, s3_sem, r3_sem, out_sem, up_sem, low_sem, x_sem, rx_sem, ry_sem,
):
    i, c, j = place()
    here = coordinates()
    barrier = pltpu.get_barrier_semaphore()
    greet(i, c, j, barrier)

    def gather_unit(u, carry):
        rows = jnp.dot(ps_ref[...], t_ref[u], preferred_element_type=jnp.float32)
        rows = rows.astype(jnp.bfloat16)
        for h in range(2):
            for k in range(4):
                snd[u, :, 4 * h + k] = rows[
                    128 * h : 128 * h + 128, 128 * k : 128 * k + 128
                ].reshape(8, 16, 128)
        last = jnp.concatenate([rows[:128, 512:], rows[128:, 512:]], axis=1)
        snd[u, :, 8] = last.reshape(8, 16, 128)
        return carry

    lax.fori_loop(0, 12, gather_unit, 0)
    pl.semaphore_wait(barrier, 71)

    def send_unit(u, k, idest, jdest):
        x = 3 * i + (12 * c + u) // 8

        @pl.when(k > 0)
        def _():
            pltpu.make_async_remote_copy(
                src_ref=snd.at[u, jdest],
                dst_ref=got.at[x, j],
                send_sem=send_sem.at[u],
                recv_sem=recv_sem.at[k],
                device_id=(2 * idest + c, jdest),
                device_id_type=MESH,
            ).start()

        @pl.when(k == 0)
        def _():
            got[x, j] = snd[u, jdest]

    def send_to(k, carry):
        idest, jdest = partner(k, 1)
        first = (idest + 4 * c) % 8
        send_unit(first, k, idest, jdest)

        @pl.when(first < 4)
        def _():
            send_unit(first + 8, k, idest, jdest)

        return carry

    lax.fori_loop(0, 64, send_to, 0)

    two = (i < 4) == (c == 0)
    sibling = (2 * i + (1 - c), j)

    def forward(k, count, core):
        isrc, jsrc = partner(k, -1)
        x = 3 * isrc + jnp.where(core == 0, 0, 3 - count)
        ref = got.at[pl.ds(x, count), jsrc]
        return ref, pltpu.make_async_remote_copy(
            src_ref=ref,
            dst_ref=ref,
            send_sem=fsend_sem.at[k],
            recv_sem=frecv_sem.at[k],
            device_id=sibling,
            device_id_type=MESH,
        )

    def pass_on(k, carry):
        def one(count):
            ref, copy = forward(k, count, c)

            @pl.when(k > 0)
            def _():
                wait_for(ref, recv_sem.at[k])

            copy.start()

        pl.when(two)(lambda: one(2))
        pl.when(jnp.logical_not(two))(lambda: one(1))
        return carry

    def accept(k, carry):
        def one(count):
            forward(k, count, 1 - c)[1].wait_recv()

        pl.when(two)(lambda: one(1))
        pl.when(jnp.logical_not(two))(lambda: one(2))
        return carry

    def finish_forward(k, carry):
        def one(count):
            forward(k, count, c)[1].wait_send()

        pl.when(two)(lambda: one(2))
        pl.when(jnp.logical_not(two))(lambda: one(1))
        return carry

    def stack_x(x):
        for h in range(2):
            for k in range(4):
                zbuf[x, 128 * h : 128 * h + 128, 128 * k : 128 * k + 128] = got[
                    x, :, 4 * h + k
                ].reshape(128, 128)
        last = got[x, :, 8].reshape(128, 128)
        zbuf[x, 0:128, 512:576] = last[:, :64]
        zbuf[x, 128:256, 512:576] = last[:, 64:]

    def stack_y(jd):
        for g in range(3):
            xs = pl.ds(8 * g, 8)
            block = jnp.concatenate(
                [
                    jnp.concatenate(
                        [got[xs, jd, 4 * h + k].reshape(128, 128) for k in range(4)], axis=1
                    )
                    for h in range(2)
                ],
                axis=0,
            )
            rows = jnp.dot(py_ref[...], block, preferred_element_type=jnp.float32)
            last = got[xs, jd, 8].reshape(128, 128)
            tail = (
                jnp.dot(py_ref[:, :128], last, preferred_element_type=jnp.float32)[:, :64]
                + jnp.dot(py_ref[:, 128:], last, preferred_element_type=jnp.float32)[:, 64:]
            )
            rows = jnp.concatenate([rows, tail], axis=1).astype(jnp.bfloat16)
            for y in range(3):
                zbuf[3 * jd + y, 80 * g : 80 * g + 80] = rows[80 * y : 80 * y + 80]
        for y in range(3):
            zbuf[3 * jd + y, 240:256] = jnp.zeros((16, PAIR), jnp.bfloat16)

    def turn(p):
        for w in range(2):
            for start, width in ((0, 256), (256, 256), (512, 64)):
                flat = lax.dot_general(
                    eye_ref[:width, :width],
                    zbuf[2 * p + w, :, start : start + width],
                    NT,
                    preferred_element_type=jnp.float32,
                )
                turned[2 * w, start : start + width] = flat[:, :128]
                turned[2 * w + 1, start : start + width] = flat[:, 128:]
        rows_at = pl.ds(pl.multiple_of(48 * p, 16), 48)
        for z in range(24):
            for half in range(2):
                cols = slice(256 * z + 128 * half, 256 * z + 128 * half + 128)
                straight = [turned[2 * w + half, 24 * z : 24 * z + 24] for w in range(2)]
                m_up[rows_at, cols] = jnp.concatenate(straight, 0).astype(jnp.bfloat16)
                strided = [turned[2 * w + half, pl.ds(z, 24, stride=24)] for w in range(2)]
                m_low[rows_at, cols] = jnp.concatenate(strided, 0).astype(jnp.bfloat16)

    def prepare(core, parity):
        at = here[0] if core == 0 else here[2]

        def per_place(n, carry):
            place_at = (at + parity + 2 * n) % 4

            def per_leg(m, carry):
                stack_x(6 * place_at + m)
                return carry

            def per_block(m, carry):
                stack_y(2 * place_at + m)
                return carry

            if core == 0:
                lax.fori_loop(0, 6, per_leg, 0)
            else:
                lax.fori_loop(0, 2, per_block, 0)

            def per_pair(m, carry):
                turn(3 * place_at + m)
                return carry

            lax.fori_loop(0, 3, per_pair, 0)
            return carry

        lax.fori_loop(0, 2, per_place, 0)

    lax.fori_loop(0, 32, pass_on, 0)
    lax.fori_loop(0, 32, accept, 0)
    pl.when(c == 0)(lambda: prepare(0, 0))
    lax.fori_loop(32, 48, pass_on, 0)
    lax.fori_loop(32, 48, accept, 0)
    pl.when(c == 1)(lambda: prepare(1, 0))
    lax.fori_loop(48, 64, pass_on, 0)
    lax.fori_loop(48, 64, accept, 0)
    pl.when(c == 0)(lambda: prepare(0, 1))
    pl.when(c == 1)(lambda: prepare(1, 1))

    def gram_panel(m, col, width):
        def step(kk, total):
            ks = pl.ds(pl.multiple_of(kk * 2048, 2048), 2048)
            return total + lax.dot_general(
                m[col:, ks], m[col : col + width, ks], NT, preferred_element_type=jnp.float32
            )

        return lax.fori_loop(0, 3, step, jnp.zeros((PAIR - col, width), jnp.float32))

    def gram(which, m):
        base = PAIR * which
        for col, width in ((0, 256), (256, 256), (512, 64)):
            q_ref[base + col : base + PAIR, col : col + width] = gram_panel(m, col, width)
            if col + width < PAIR:
                below = q_ref[base + col + width : base + PAIR, col : col + width]
                q_ref[base + col : base + col + width, col + width :] = below.T

    scale = 1.0 / CHI**3

    def moved(axis, to):
        to_coords = [to if a == axis else here[a] for a in range(3)]
        di, dj = chip_at(*to_coords)
        return 2 * di + c, dj

    def axes(part):
        return part, (part + 1) % 3, (part + 2) % 3

    def others(axis, body):
        def one(s, carry):
            body((here[axis] + s) % 4)
            return carry

        lax.fori_loop(1, 4, one, 0)

    def four(part, to):
        return pl.ds(pl.multiple_of(24 * (16 * part + 4 * to), 8), 96)

    def stage1(part):
        first = axes(part)[0]

        def send(to):
            pltpu.make_async_remote_copy(
                src_ref=q_ref.at[four(part, to)],
                dst_ref=parts1.at[part, here[first]],
                send_sem=s1_sem.at[part],
                recv_sem=r1_sem.at[part],
                device_id=moved(first, to),
                device_id_type=MESH,
            ).start()

        others(first, send)
        parts1[part, here[first]] = q_ref[four(part, here[first])]

    gram(0, m_up)
    stage1(0)
    gram(1, m_low)
    stage1(1)
    stage1(2)

    for part in range(3):
        second = axes(part)[1]
        take(parts1.at[part], 3, r1_sem.at[part])
        total = (parts1[part, 0] + parts1[part, 1]) + (parts1[part, 2] + parts1[part, 3])
        sums1[part] = total.reshape(4, CHI, PAIR)

        def send(to, part=part, second=second):
            pltpu.make_async_remote_copy(
                src_ref=sums1.at[part, to],
                dst_ref=parts2.at[part, here[second]],
                send_sem=s2_sem.at[part],
                recv_sem=r2_sem.at[part],
                device_id=moved(second, to),
                device_id_type=MESH,
            ).start()

        others(second, send)
        parts2[part, here[second]] = sums1[part, here[second]]

    owned = (here[0] + here[1] + here[2]) % 4
    for part in range(3):
        third = axes(part)[2]
        take(parts2.at[part], 3, r2_sem.at[part])
        sums2[part] = (parts2[part, 0] + parts2[part, 1]) + (parts2[part, 2] + parts2[part, 3])

        @pl.when(owned == part)
        def _(part=part, third=third):
            parts3[here[third]] = sums2[part]

        @pl.when(owned != part)
        def _(part=part, third=third):
            to = (part + 8 - here[axes(part)[0]] - here[axes(part)[1]]) % 4
            pltpu.make_async_remote_copy(
                src_ref=sums2.at[part],
                dst_ref=parts3.at[here[third]],
                send_sem=s3_sem.at[part],
                recv_sem=r3_sem,
                device_id=moved(third, to),
                device_id_type=MESH,
            ).start()

    unit = 16 * owned + 4 * jnp.where(
        owned == 0, here[0], jnp.where(owned == 1, here[1], here[2])
    ) + jnp.where(owned == 0, here[1], jnp.where(owned == 1, here[2], here[0]))
    owner = owned < 3

    @pl.when(owner)
    def _():
        wait_for(parts3.at[pl.ds(0, 3)], r3_sem)
        total = (parts3[0] + parts3[1]) + (parts3[2] + parts3[3])
        mine[...] = relayout(total * scale, st_ref, mask_ref)

    is_up = jnp.logical_and(owner, unit < 24)
    is_low = jnp.logical_and(owner, unit >= 24)
    local = jnp.where(is_up, unit, unit - 24)
    by_i = is_up == (c == 0)
    block = local // 3
    keeps = jnp.logical_and(owner, jnp.where(by_i, i, j) == block)

    def deliver(slots, sem):
        def one(s, carry):
            other = jnp.where(by_i, (j + s) % 8, (i + s) % 8)
            di = jnp.where(by_i, block, other)
            dj = jnp.where(by_i, other, block)
            same = jnp.logical_and(di == i, dj == j)

            @pl.when(jnp.logical_not(same))
            def _():
                pltpu.make_async_remote_copy(
                    src_ref=mine,
                    dst_ref=slots.at[local % 3],
                    send_sem=out_sem,
                    recv_sem=sem,
                    device_id=(2 * di + c, dj),
                    device_id_type=MESH,
                ).start()

            @pl.when(same)
            def _():
                slots[local % 3] = mine[...]

            return carry

        lax.fori_loop(0, 8, one, 0)

    @pl.when(is_up)
    def _():
        deliver(ups, up_sem)

    @pl.when(is_low)
    def _():
        deliver(lows, low_sem)

    def take_rows(slots, kept, sem):
        @pl.when(kept)
        def _():
            take(slots, 2, sem)

        @pl.when(jnp.logical_not(kept))
        def _():
            take(slots, 3, sem)

    take_rows(ups, jnp.logical_and(keeps, is_up), up_sem)
    take_rows(lows, jnp.logical_and(keeps, is_low), low_sem)

    piece[...] = lax.dot_general(
        ups[...].reshape(72, PAIR), lows[...].reshape(72, PAIR), NT,
        precision=HIGHEST, preferred_element_type=jnp.float32,
    ) * scale

    def spread(out_ref, slot, sem):
        def one(s, carry):
            core = (c + s) % 2
            other = s // 2
            di = jnp.where(c == 0, i, (i + other) % 8)
            dj = jnp.where(c == 0, (j + other) % 8, j)
            pltpu.make_async_remote_copy(
                src_ref=piece,
                dst_ref=out_ref.at[slot],
                send_sem=x_sem.at[s % 2],
                recv_sem=sem,
                device_id=(2 * di + core, dj),
                device_id_type=MESH,
            ).start()
            return carry

        lax.fori_loop(1, 16, one, 0)
        out_ref[slot] = piece[...]

    @pl.when(c == 0)
    def _():
        spread(ox_ref, j, rx_sem)

    @pl.when(c == 1)
    def _():
        spread(oy_ref, i, ry_sem)

    for part in range(3):
        take(parts1.at[part], 3, s1_sem.at[part])
        wait_for(sums1.at[part, pl.ds(0, 3)], s2_sem.at[part])

        @pl.when(owned != part)
        def _(part=part):
            wait_for(sums2.at[part], s3_sem.at[part])

    @pl.when(keeps)
    def _():
        wait_for(q_ref.at[pl.ds(0, 7 * CHI)], out_sem)

    @pl.when(jnp.logical_and(owner, jnp.logical_not(keeps)))
    def _():
        wait_for(q_ref.at[pl.ds(0, 8 * CHI)], out_sem)

    lax.fori_loop(0, 64, finish_forward, 0)

    def drain(u, carry):
        idest = (12 * c + u) % 8
        pl.when(idest == i)(lambda: take(snd.at[u], 7, send_sem.at[u]))
        pl.when(idest != i)(lambda: take(snd.at[u], 8, send_sem.at[u]))
        return carry

    lax.fori_loop(0, 12, drain, 0)

    take(ox_ref, 7, x_sem.at[0])
    take(ox_ref, 8, x_sem.at[1])

    @pl.when(c == 0)
    def _():
        take(ox_ref, 7, rx_sem)
        take(oy_ref, 8, ry_sem)

    @pl.when(c == 1)
    def _():
        take(ox_ref, 8, rx_sem)
        take(oy_ref, 7, ry_sem)


def per_device(tensor, trial_x, trial_y):
    vmem = pl.BlockSpec(memory_space=pltpu.VMEM)
    dma = pltpu.SemaphoreType.DMA
    index = np.arange(PAIR)
    tile = (index[:, None] % CHI == index[None, :] % CHI).astype(np.float32)
    mask = (np.arange(CHI)[:, None] == index[None, :] // CHI).astype(np.float32)
    f32, bf16 = jnp.float32, jnp.bfloat16
    out_x, out_y = pl.pallas_call(
        fused_kernel,
        out_shape=[jax.ShapeDtypeStruct((8, 72, 72), f32)] * 2,
        in_specs=[vmem] * 6,
        out_specs=[vmem] * 2,
        scratch_shapes=[
            pltpu.VMEM((12, 8, 9, 16, 128), bf16),
            pltpu.VMEM((24, 8, 9, 16, 128), bf16),
            pltpu.VMEM((24, STACK, PAIR), bf16),
            pltpu.VMEM((4, PAIR, 128), f32),
            pltpu.VMEM((PAIR, 24 * 256), bf16),
            pltpu.VMEM((PAIR, 24 * 256), bf16),
            pltpu.VMEM((2 * PAIR, PAIR), f32),
            dma((12,)), dma((64,)), dma((64,)), dma((64,)),
            pltpu.VMEM((3, 4, 4 * CHI, PAIR), f32),
            pltpu.VMEM((3, 4, CHI, PAIR), f32),
            pltpu.VMEM((4, CHI, PAIR), f32),
            pltpu.VMEM((3, 4, CHI, PAIR), f32),
            pltpu.VMEM((3, CHI, PAIR), f32),
            pltpu.VMEM((CHI, PAIR), f32),
            pltpu.VMEM((3, CHI, PAIR), f32),
            pltpu.VMEM((3, CHI, PAIR), f32),
            pltpu.VMEM((72, 72), f32),
            dma((3,)), dma((3,)), dma((3,)), dma((3,)), dma((3,)),
            dma, dma, dma, dma, dma((2,)), dma, dma,
        ],
        compiler_params=pltpu.CompilerParams(
            collective_id=0, has_side_effects=True, vmem_limit_bytes=62 * 2**20
        ),
        name="hotrg_step",
    )(
        tensor.reshape(12, 216, PAIR),
        jnp.asarray(send_rows(), bf16),
        jnp.asarray(y_rows(), bf16),
        jnp.asarray(np.eye(256), bf16),
        jnp.asarray(tile, bf16),
        jnp.asarray(mask, f32),
    )

    def merged(out):
        return out.reshape(8, 3, CHI, 3, CHI).transpose(1, 0, 3, 2, 4).reshape(72, PAIR)

    core = lax.axis_index("aa") % 2
    gram_x = lax.dynamic_slice_in_dim(merged(out_x), core * 36, 36, 0)
    gram_y = merged(out_y)
    proj_x = jnp.dot(gram_x, trial_x, precision=HIGHEST, preferred_element_type=jnp.float32)
    proj_y = jnp.dot(gram_y, trial_y, precision=HIGHEST, preferred_element_type=jnp.float32)
    return (gram_x, proj_x, gram_y, proj_y)


def solution(mesh):
    in_specs = (P("aa", "ba", None), P(), P())
    out_specs = (P("aa", None), P("aa", None), P("ba", None), P("ba", None))
    return jax.shard_map(
        per_device, mesh=mesh, in_specs=in_specs, out_specs=out_specs, check_vma=False
    )
```

time: 170 us -> 134 us (0.79)
  Pallas kernels: 164 us -> 128 us
    pallas_call x2 -> x1, Pallas kernels: 164 us -> 128 us  [per_device(): pl.pallas_call(fused_kernel, out_shape=[jax.ShapeDtypeStruct((8, 72, 72),...]
where the time goes in v3:
time: 134 us
  Pallas kernels  128 us (96%)
  local copies, waits for them, and re-layouts  3.08 us (2%)
  matrix products  1.72 us (1%)
    pallas_call x1, Pallas kernels, per_device(): pl.pallas_call(fused_kernel, out_shape=[jax.ShapeDtypeStruct((8, 72, 72),...  128 us

profile of v3, /device:TPU:1, one launch (start us, length us, event | category | flops | bytes accessed | tf_op | source)
XLA Modules:
  0.0 134.0 jit_solution(446445764898600164)
XLA Ops:
  0.6 0.0 copy-start
  0.6 128.4 %hotrg_step.1 = (f32[8,72,72]{2,1,0:T(8,128)}, f32[8,72,72]{2,1,0:T(8,128)}) custom-call(bf16[12,216,576]{2,1,0:T(8,128)(2,1)} %bitcast.13, bf16[256,216]{1,0:T(8,128)(2,1)} %constant.34.clone.ps_ref, bf16[240,256]{1,0:T(8,128)(2,1)} %constant.35.clone.py_ref, bf16[256,256]{1,0:T(8,128)(2,1)} %constant.36.clone.eye_ref, ...), custom_call_target="tpu_custom_call" | custom-call | tf_op jit(solution)/shard_map/hotrg_step/pallas_call | solution.py:559
  129.1 1.5 %reshape.24 = f32[8,3,24,3,24]{4,3,2,1,0:T(4,128)S(1)} reshape(f32[8,72,72]{2,1,0:T(8,128)} %get-tuple-element.6) | data formatting | bytes 331776 | tf_op jit(solution)/shard_map/reshape | solution.py:599
  130.6 0.0 copy-start.4
  130.6 0.1 copy.14
  130.7 0.0 copy-start.3
  130.7 0.3 reshape.25
  131.0 0.4 copy-done.4
  131.4 0.0 copy-start.2
  131.4 0.8 fusion
  132.3 0.0 copy-done.3
  132.3 0.4 reshape.26
  132.7 0.1 copy.15
  132.8 0.0 copy-done.2
  132.8 0.3 reshape.27
  133.1 0.0 copy-done
  133.1 0.0 copy-start.1
  133.1 0.9 fusion.1
  134.0 0.0 copy-done.1
  (1 shorter events, 0.0 us)
Async XLA Ops:
  0.6 132.4 %copy-start = (f32[576,24]{0,1:T(8,128)S(1)}, f32[576,24]{0,1:T(8,128)}, u32[]{:S(2)}) copy-start(f32[576,24]{0,1:T(8,128)} %param.10) | copy-start | bytes 165892
  130.6 0.8 copy-start.4
  130.7 1.6 %copy-start.3 = (f32[8,72,72]{2,1,0:T(8,128)S(1)}, f32[8,72,72]{2,1,0:T(8,128)}, u32[]{:S(2)}) copy-start(f32[8,72,72]{2,1,0:T(8,128)} %get-tuple-element.7) | copy-start | bytes 497668
  131.4 1.3 %copy-start.2 = (f32[36,576]{1,0:T(8,128)}, f32[36,576]{1,0:T(8,128)S(1)}, u32[]{:S(2)}) copy-start(f32[36,576]{1,0:T(8,128)S(1)} %constant_dynamic-slice_fusion) | copy-start | bytes 248836
  133.1 0.9 copy-start.1

commit v4 on v3

v4 whole, which is shorter than its diff:
```python
import functools

import jax
import jax.numpy as jnp
import numpy as np
from jax import lax
from jax.experimental import pallas as pl
from jax.experimental.pallas import tpu as pltpu
from jax.sharding import PartitionSpec as P

CHI = 24
PAIR = 576
GROUPS = 8
MSG = 32
STACK = GROUPS * MSG
HIGHEST = lax.Precision.HIGHEST
MESH = pl.DeviceIdType.MESH
NT = (((1,), (1,)), ((), ()))


def send_rows():
    out = np.zeros((STACK, 216), np.float32)
    for jd in range(8):
        for xs in range(3):
            for y in range(3):
                for ys in range(3):
                    h, r = divmod(xs * 9 + y * 3 + ys, 16)
                    out[h * 128 + jd * 16 + r, xs * 72 + y * 24 + jd * 3 + ys] = 1
    return out


def y_rows():
    out = np.zeros((192, 192), np.float32)
    for xg in range(6):
        for xs in range(3):
            for y in range(3):
                for ys in range(3):
                    h, r = divmod(xs * 9 + y * 3 + ys, 16)
                    out[y * 64 + xg * 9 + xs * 3 + ys, h * 96 + xg * 16 + r] = 1
    return out


def place():
    aa = lax.axis_index("aa")
    ba = lax.axis_index("ba")
    return aa // 2, aa % 2, ba


def coordinates():
    aa = lax.axis_index("aa")
    ba = lax.axis_index("ba")
    return aa // 4, (aa // 2) % 2 + 2 * (ba % 2), ba // 2


def chip_at(z, x, y):
    return 2 * z + x % 2, 2 * y + x // 2


def shift_of(k):
    quarter, rest = k // 16, k % 16
    low, high = rest % 4, rest // 4
    dz = 2 * (low % 2) + quarter // 2
    dx = (low + high) % 4
    dy = 2 * ((high + low // 2) % 2) + quarter % 2
    return dz, dx, dy


def partner(k, sign):
    z, x, y = coordinates()
    dz, dx, dy = shift_of(k)
    return chip_at((z + 4 + sign * dz) % 4, (x + 4 + sign * dx) % 4, (y + 4 + sign * dy) % 4)


def wait_for(ref, sem):
    pltpu.make_async_copy(ref, ref, sem).wait()


def take(ref, count, sem):
    wait_for(ref.at[pl.ds(0, count)], sem)


def greet(i, c, j, barrier):
    def one(n, carry):
        di, dj = n // 8, n % 8

        @pl.when(jnp.logical_not(jnp.logical_and(di == i, dj == j)))
        def _():
            pl.semaphore_signal(barrier, inc=1, device_id=(2 * di + c, dj), device_id_type=MESH)

        return carry

    lax.fori_loop(0, 64, one, 0)

    @pl.when(c == 0)
    def _():
        pl.semaphore_signal(barrier, inc=1, device_id=(2 * i + 1, j), device_id_type=MESH)

    @pl.when(c == 1)
    def _():
        def across(n, carry):
            pl.semaphore_signal(barrier, inc=1, device_id=(2 * i, n), device_id_type=MESH)
            return carry

        lax.fori_loop(0, 8, across, 0)


def relayout(block, st_ref, mask_ref):
    spread = jnp.concatenate([block[:, CHI * q : CHI * q + CHI] for q in range(CHI)], axis=0)
    high = spread.astype(jnp.bfloat16)
    rest = spread - high.astype(jnp.float32)
    mid = rest.astype(jnp.bfloat16)
    low = (rest - mid.astype(jnp.float32)).astype(jnp.bfloat16)
    st = st_ref[...]
    tiled = (
        jnp.dot(high, st, preferred_element_type=jnp.float32)
        + jnp.dot(mid, st, preferred_element_type=jnp.float32)
        + jnp.dot(low, st, preferred_element_type=jnp.float32)
    )
    return jnp.sum(tiled.reshape(CHI, CHI, PAIR) * mask_ref[...][None, :, :], axis=1)


def unit_of(part, kind, g, e):
    if part == 0:
        hi, lo = g, e
    elif part == 1:
        hi, lo = (2 * (g % 2) + e, g // 2) if kind else (2 * (g // 2) + e, g % 2)
    else:
        hi, lo = (g, e) if kind else (2 * (g // 2) + e, g % 2)
    return 6 * hi + 3 * lo + part


def second_place(part, kind, g, e):
    if part == 0:
        return 1 + e if kind else 3 * e
    half = (g % 2 if kind else 1 - g % 2) if part == 1 else (1 - g // 2 if kind else g // 2)
    return 2 * half + e


def owned_unit(part, g, m):
    if part == 0:
        kind = (m == 1) | (m == 2)
        return kind, jnp.where(kind, g, (g + 2 * m + 3) % 4)
    if part == 1:
        kind = m // 2 == g % 2
        return kind, jnp.where(kind, (2 * g + 3 * m + 2) % 4, 2 * (g // 2) + m % 2)
    kind = m // 2 != g // 2
    return kind, jnp.where(kind, 2 * (m % 2) + (m + 1) % 2, g % 2 + 2 * (m % 2))


def fused_kernel(
    t_ref, ps_ref, py_ref, eye_ref, st_ref, mask_ref, ox_ref, oy_ref,
    snd, got, zbuf, turned, m_up, m_low, q_ref,
    send_sem, recv_sem, fsend_sem, frecv_sem,
    parts1, parts2, parts3, sums1, sums2, mine, rows_ab, piece,
    s1_sem, r1_sem, s2_sem, r2_sem, s3_sem, r3_sem, out_sem, rows_sem, x_sem, rx_sem, y_sem, ry_sem,
    both_sem,
):
    i, c, j = place()
    here = coordinates()
    barrier = pltpu.get_barrier_semaphore()
    greet(i, c, j, barrier)

    def gather_unit(u, carry):
        rows = jnp.dot(ps_ref[...], t_ref[u], preferred_element_type=jnp.float32)
        rows = rows.astype(jnp.bfloat16)
        for h in range(2):
            for k in range(4):
                snd[u, :, 4 * h + k] = rows[
                    128 * h : 128 * h + 128, 128 * k : 128 * k + 128
                ].reshape(8, 16, 128)
        last = jnp.concatenate([rows[:128, 512:], rows[128:, 512:]], axis=1)
        snd[u, :, 8] = last.reshape(8, 16, 128)
        return carry

    lax.fori_loop(0, 12, gather_unit, 0)
    pl.when(c == 0)(lambda: pl.semaphore_wait(barrier, 71))
    pl.when(c == 1)(lambda: pl.semaphore_wait(barrier, 64))

    def send_unit(u, k, idest, jdest):
        x = 3 * i + (12 * c + u) // 8

        @pl.when(k > 0)
        def _():
            pltpu.make_async_remote_copy(
                src_ref=snd.at[u, jdest],
                dst_ref=got.at[x, j],
                send_sem=send_sem.at[u],
                recv_sem=recv_sem.at[k],
                device_id=(2 * idest + c, jdest),
                device_id_type=MESH,
            ).start()

        @pl.when(k == 0)
        def _():
            got[x, j] = snd[u, jdest]

    def send_to(k, carry):
        idest, jdest = partner(k, 1)
        first = (idest + 4 * c) % 8
        send_unit(first, k, idest, jdest)

        @pl.when(first < 4)
        def _():
            send_unit(first + 8, k, idest, jdest)

        return carry

    lax.fori_loop(0, 64, send_to, 0)

    two = (i < 4) == (c == 0)
    sibling = (2 * i + (1 - c), j)

    def forward(k, count, core):
        isrc, jsrc = partner(k, -1)
        x = 3 * isrc + jnp.where(core == 0, 0, 3 - count)
        ref = got.at[pl.ds(x, count), jsrc]
        return ref, pltpu.make_async_remote_copy(
            src_ref=ref,
            dst_ref=ref,
            send_sem=fsend_sem.at[k],
            recv_sem=frecv_sem.at[k],
            device_id=sibling,
            device_id_type=MESH,
        )

    def pass_on(k, carry):
        def one(count):
            ref, copy = forward(k, count, c)

            @pl.when(k > 0)
            def _():
                wait_for(ref, recv_sem.at[k])

            copy.start()

        pl.when(two)(lambda: one(2))
        pl.when(jnp.logical_not(two))(lambda: one(1))
        return carry

    def accept(k, carry):
        def one(count):
            forward(k, count, 1 - c)[1].wait_recv()

        pl.when(two)(lambda: one(1))
        pl.when(jnp.logical_not(two))(lambda: one(2))
        return carry

    def finish_forward(k, carry):
        def one(count):
            forward(k, count, c)[1].wait_send()

        pl.when(two)(lambda: one(2))
        pl.when(jnp.logical_not(two))(lambda: one(1))
        return carry

    def far(axis, parity, n):
        return (here[axis] + parity + 2 * n) % 4

    def stack_x(x, half):
        for n in range(2):
            js = pl.ds(2 * far(2, half, n), 2)
            for h in range(2):
                at = slice(64 * h + 32 * n, 64 * h + 32 * n + 32)
                for k in range(4):
                    zbuf[x, half, at, 128 * k : 128 * k + 128] = got[x, js, 4 * h + k].reshape(
                        32, 128
                    )
            last = got[x, js, 8].reshape(32, 128)
            zbuf[x, half, 32 * n : 32 * n + 32, 512:576] = last[:, :64]
            zbuf[x, half, 64 + 32 * n : 96 + 32 * n, 512:576] = last[:, 64:]

    def stack_y(jd, half):
        for n in range(2):
            xs = pl.ds(6 * far(0, half, n), 6)
            block = jnp.concatenate(
                [
                    jnp.concatenate(
                        [got[xs, jd, 4 * h + k].reshape(96, 128) for k in range(4)], axis=1
                    )
                    for h in range(2)
                ],
                axis=0,
            )
            rows = jnp.dot(py_ref[...], block, preferred_element_type=jnp.float32)
            last = got[xs, jd, 8].reshape(96, 128)
            tail = (
                jnp.dot(py_ref[:, :96], last, preferred_element_type=jnp.float32)[:, :64]
                + jnp.dot(py_ref[:, 96:], last, preferred_element_type=jnp.float32)[:, 64:]
            )
            rows = jnp.concatenate([rows, tail], axis=1).astype(jnp.bfloat16)
            for y in range(3):
                zbuf[3 * jd + y, half, 64 * n : 64 * n + 64] = rows[64 * y : 64 * y + 64]

    def turn(p, half):
        for w in range(2):
            for start, width in ((0, 256), (256, 256), (512, 64)):
                turned[w, start : start + width] = lax.dot_general(
                    eye_ref[:width, :width],
                    zbuf[2 * p + w, half, :, start : start + width],
                    NT,
                    preferred_element_type=jnp.float32,
                )
        rows_at = pl.ds(pl.multiple_of(48 * p, 16), 48)
        for z in range(24):
            cols = slice(128 * z, 128 * z + 128)
            straight = [turned[w, 24 * z : 24 * z + 24] for w in range(2)]
            m_up[half, rows_at, cols] = jnp.concatenate(straight, 0).astype(jnp.bfloat16)
            strided = [turned[w, pl.ds(z, 24, stride=24)] for w in range(2)]
            m_low[half, rows_at, cols] = jnp.concatenate(strided, 0).astype(jnp.bfloat16)

    def prepare(legs, half, meanwhile):
        for n in range(2):
            @pl.when(c == 0)
            def _(n=n):
                at = far(0, legs, n)

                def per_leg(m, carry):
                    stack_x(6 * at + m, half)
                    return carry

                lax.fori_loop(0, 6, per_leg, 0)

            @pl.when(c == 1)
            def _(n=n):
                at = far(2, legs, n)

                def per_leg(m, carry):
                    stack_y(2 * at + m, half)
                    return carry

                lax.fori_loop(0, 2, per_leg, 0)

            at = jnp.where(c == 0, far(0, legs, n), far(2, legs, n))

            def per_pair(m, carry):
                turn(3 * at + m, half)
                return carry

            lax.fori_loop(0, 3, per_pair, 0)
            meanwhile(n)

    panels = ((0, 256), (256, 256), (512, 64))

    def gram(which, m, half):
        base = PAIR * which
        for col, width in panels:
            total = lax.dot_general(
                m[half, col:, :1536], m[half, col : col + width, :1536],
                NT, preferred_element_type=jnp.float32,
            )
            total += lax.dot_general(
                m[half, col:, 1536:], m[half, col : col + width, 1536:],
                NT, preferred_element_type=jnp.float32,
            )
            if half:
                total += q_ref[base + col : base + PAIR, col : col + width]
            q_ref[base + col : base + PAIR, col : col + width] = total
            if half and col + width < PAIR:
                below = q_ref[base + col + width : base + PAIR, col : col + width]
                q_ref[base + col : base + col + width, col + width :] = below.T

    def passing(start, stop):
        lax.fori_loop(start, stop, pass_on, 0)

    def accepting(start, stop):
        lax.fori_loop(start, stop, accept, 0)

    passing(0, 16)
    accepting(0, 16)
    prepare(0, 0, lambda n: passing(16 + 8 * n, 24 + 8 * n))
    accepting(16, 32)

    @pl.when(c == 0)
    def _():
        prepare(0, 1, lambda n: passing(32 + 8 * n, 40 + 8 * n))

    @pl.when(c == 1)
    def _():
        prepare(1, 0, lambda n: passing(32 + 4 * n, 36 + 4 * n))
        gram(0, m_up, 0)
        passing(40, 44)
        gram(1, m_low, 0)
        passing(44, 48)

    accepting(32, 48)

    @pl.when(c == 0)
    def _():
        prepare(1, 0, lambda n: passing(48 + 4 * n, 52 + 4 * n))
        gram(0, m_up, 0)
        passing(56, 60)
        gram(1, m_low, 0)
        passing(60, 64)

    @pl.when(c == 1)
    def _():
        prepare(0, 1, lambda n: passing(48 + 8 * n, 56 + 8 * n))

    accepting(48, 64)
    prepare(1, 1, lambda n: None)

    scale = 1.0 / CHI**3

    def moved(axis, to):
        to_coords = [to if a == axis else here[a] for a in range(3)]
        di, dj = chip_at(*to_coords)
        return 2 * di + c, dj

    def axes(part):
        return part, (part + 1) % 3, (part + 2) % 3

    def stage1(which):
        for part in range(3):
            first = axes(part)[0]
            at = here[first]

            def rows(to, e, part=part):
                n = jnp.where(c == which, unit_of(part, 0, to, e), unit_of(part, 1, to, e))
                return pl.ds(pl.multiple_of(PAIR * which + CHI * n, 8), CHI)

            def send(step, carry, part=part, first=first, at=at, rows=rows):
                to = (at + step) % 4
                for e in range(2):
                    pltpu.make_async_remote_copy(
                        src_ref=q_ref.at[rows(to, e)],
                        dst_ref=parts1.at[part, which, at, e],
                        send_sem=s1_sem.at[part, which],
                        recv_sem=r1_sem.at[part, which],
                        device_id=moved(first, to),
                        device_id_type=MESH,
                    ).start()
                return carry

            lax.fori_loop(1, 4, send, 0)
            for e in range(2):
                parts1[part, which, at, e] = q_ref[rows(at, e)]

    def stage2(which):
        for part in range(3):
            first, second, _ = axes(part)
            g, at = here[first], here[second]
            ref = parts1.at[part, which]
            take(ref, 3, r1_sem.at[part, which])
            sums1[part, which] = (ref[0] + ref[1]) + (ref[2] + ref[3])
            for e in range(2):
                to = jnp.where(
                    c == which, second_place(part, 0, g, e), second_place(part, 1, g, e)
                )

                @pl.when(to != at)
                def _(part=part, second=second, at=at, to=to, e=e):
                    pltpu.make_async_remote_copy(
                        src_ref=sums1.at[part, which, e],
                        dst_ref=parts2.at[part, at],
                        send_sem=s2_sem.at[part],
                        recv_sem=r2_sem.at[part],
                        device_id=moved(second, to),
                        device_id_type=MESH,
                    ).start()

                @pl.when(to == at)
                def _(part=part, at=at, e=e):
                    parts2[part, at] = sums1[part, which, e]

    gram(0, m_up, 1)
    stage1(0)
    gram(1, m_low, 1)
    stage1(1)
    stage2(0)
    stage2(1)

    owner = []
    for part in range(3):
        first, second, third = axes(part)
        kind, to = owned_unit(part, here[first], here[second])
        at = here[third]
        owner.append((kind, to == at))
        take(parts2.at[part], 3, r2_sem.at[part])
        total = (parts2[part, 0] + parts2[part, 1]) + (parts2[part, 2] + parts2[part, 3])

        @pl.when(to == at)
        def _(part=part, at=at, total=total):
            parts3[part, at] = total

        @pl.when(to != at)
        def _(part=part, third=third, at=at, to=to, total=total):
            sums2[part] = total
            pltpu.make_async_remote_copy(
                src_ref=sums2.at[part],
                dst_ref=parts3.at[part, at],
                send_sem=s3_sem.at[part],
                recv_sem=r3_sem.at[part],
                device_id=moved(third, to),
                device_id_type=MESH,
            ).start()

    for part in range(3):
        kind, owns = owner[part]
        which = jnp.where(kind, 1 - c, c)

        @pl.when(owns)
        def _(part=part, kind=kind, which=which):
            take(parts3.at[part], 3, r3_sem.at[part])
            total = (parts3[part, 0] + parts3[part, 1]) + (parts3[part, 2] + parts3[part, 3])
            mine[part] = relayout(total * scale, st_ref, mask_ref)

            def give(step, carry):
                di = jnp.where(kind, (i + step) % 8, i)
                dj = jnp.where(kind, j, (j + step) % 8)
                pltpu.make_async_remote_copy(
                    src_ref=mine.at[part],
                    dst_ref=rows_ab.at[which, part],
                    send_sem=out_sem.at[part],
                    recv_sem=rows_sem.at[which, part],
                    device_id=(2 * di + c, dj),
                    device_id_type=MESH,
                ).start()
                return carry

            lax.fori_loop(1, 8, give, 0)
            rows_ab[which, part] = mine[part]

    for part in range(3):
        kind, owns = owner[part]
        for which in range(2):
            own = jnp.logical_and(owns, kind == (c != which))

            @pl.when(jnp.logical_not(own))
            def _(part=part, which=which):
                wait_for(rows_ab.at[which, part], rows_sem.at[which, part])

    product = lax.dot_general(
        rows_ab[0].reshape(72, PAIR), rows_ab[1].reshape(72, PAIR), NT,
        precision=HIGHEST, preferred_element_type=jnp.float32,
    ) * scale
    for a in range(3):
        piece[a] = product[CHI * a : CHI * a + CHI]

    def spread_x(first_two):
        for core in range(2):
            count = 2 if first_two == (core == 0) else 1
            start = 0 if core == 0 else 3 - count
            slot = 2 * j + (0 if core == 0 else 2 - count)
            source = piece.at[pl.ds(start, count)]
            target = ox_ref.at[pl.ds(slot, count)]

            def one(step, carry, core=core, source=source, target=target):
                pltpu.make_async_remote_copy(
                    src_ref=source,
                    dst_ref=target,
                    send_sem=x_sem.at[core],
                    recv_sem=rx_sem,
                    device_id=(2 * i + core, (j + step) % 8),
                    device_id_type=MESH,
                ).start()
                return carry

            lax.fori_loop(1 if core == 0 else 0, 8, one, 0)
            if core == 0:
                for a in range(count):
                    ox_ref[slot + a] = piece[start + a]

    swap = pltpu.make_async_remote_copy(
        src_ref=oy_ref,
        dst_ref=oy_ref,
        send_sem=both_sem.at[0],
        recv_sem=both_sem.at[1],
        device_id=(2 * i, j),
        device_id_type=MESH,
    )

    @pl.when(jnp.logical_and(c == 0, j < 4))
    def _():
        spread_x(True)

    @pl.when(jnp.logical_and(c == 0, j >= 4))
    def _():
        spread_x(False)

    @pl.when(c == 1)
    def _():
        def one(step, carry):
            pltpu.make_async_remote_copy(
                src_ref=piece,
                dst_ref=oy_ref.at[i],
                send_sem=y_sem,
                recv_sem=ry_sem,
                device_id=(2 * ((i + step) % 8) + 1, j),
                device_id_type=MESH,
            ).start()
            return carry

        lax.fori_loop(1, 8, one, 0)
        oy_ref[i] = piece[...]
        take(oy_ref, 7, ry_sem)
        swap.start()

    for part in range(3):
        for which in range(2):
            take(parts1.at[part, which], 3, s1_sem.at[part, which])
        take(parts2.at[part], 3, s2_sem.at[part])
        owns = owner[part][1]
        pl.when(jnp.logical_not(owns))(
            lambda part=part: wait_for(sums2.at[part], s3_sem.at[part])
        )
        pl.when(owns)(
            lambda part=part: wait_for(q_ref.at[pl.ds(0, 7 * CHI)], out_sem.at[part])
        )

    lax.fori_loop(0, 64, finish_forward, 0)

    def drain(u, carry):
        idest = (12 * c + u) % 8
        pl.when(idest == i)(lambda: take(snd.at[u], 7, send_sem.at[u]))
        pl.when(idest != i)(lambda: take(snd.at[u], 8, send_sem.at[u]))
        return carry

    lax.fori_loop(0, 12, drain, 0)

    @pl.when(jnp.logical_and(c == 0, j < 4))
    def _():
        take(ox_ref, 14, x_sem.at[0])
        take(ox_ref, 8, x_sem.at[1])
        take(ox_ref, 10, rx_sem)

    @pl.when(jnp.logical_and(c == 0, j >= 4))
    def _():
        take(ox_ref, 7, x_sem.at[0])
        take(ox_ref, 16, x_sem.at[1])
        take(ox_ref, 11, rx_sem)

    @pl.when(c == 0)
    def _():
        swap.wait_recv()

    @pl.when(c == 1)
    def _():
        take(ox_ref, 12, rx_sem)
        take(oy_ref, 7, y_sem)
        swap.wait_send()


def per_device(tensor, trial_x, trial_y):
    vmem = pl.BlockSpec(memory_space=pltpu.VMEM)
    dma = pltpu.SemaphoreType.DMA
    index = np.arange(PAIR)
    tile = (np.arange(CHI)[:, None] == index[None, :] % CHI).astype(np.float32)
    mask = (np.arange(CHI)[:, None] == index[None, :] // CHI).astype(np.float32)
    f32, bf16 = jnp.float32, jnp.bfloat16
    out_x, out_y = pl.pallas_call(
        fused_kernel,
        out_shape=[
            jax.ShapeDtypeStruct((16, CHI, 72), f32),
            jax.ShapeDtypeStruct((8, 3, CHI, 72), f32),
        ],
        in_specs=[vmem] * 6,
        out_specs=[vmem] * 2,
        scratch_shapes=[
            pltpu.VMEM((12, 8, 9, 16, 128), bf16),
            pltpu.VMEM((24, 8, 9, 16, 128), bf16),
            pltpu.VMEM((24, 2, 128, PAIR), bf16),
            pltpu.VMEM((2, PAIR, 128), f32),
            pltpu.VMEM((2, PAIR, 24 * 128), bf16),
            pltpu.VMEM((2, PAIR, 24 * 128), bf16),
            pltpu.VMEM((2 * PAIR, PAIR), f32),
            dma((12,)), dma((64,)), dma((64,)), dma((64,)),
            pltpu.VMEM((3, 2, 4, 2, CHI, PAIR), f32),
            pltpu.VMEM((3, 4, CHI, PAIR), f32),
            pltpu.VMEM((3, 4, CHI, PAIR), f32),
            pltpu.VMEM((3, 2, 2, CHI, PAIR), f32),
            pltpu.VMEM((3, CHI, PAIR), f32),
            pltpu.VMEM((3, CHI, PAIR), f32),
            pltpu.VMEM((2, 3, CHI, PAIR), f32),
            pltpu.VMEM((3, CHI, 72), f32),
            dma((3, 2)), dma((3, 2)), dma((3,)), dma((3,)), dma((3,)), dma((3,)),
            dma((3,)), dma((2, 3)), dma((2,)), dma, dma, dma, dma((2,)),
        ],
        compiler_params=pltpu.CompilerParams(
            collective_id=0, has_side_effects=True, vmem_limit_bytes=62 * 2**20
        ),
        name="hotrg_step",
    )(
        tensor.reshape(12, 216, PAIR),
        jnp.asarray(send_rows(), bf16),
        jnp.asarray(y_rows(), bf16),
        jnp.asarray(np.eye(256), bf16),
        jnp.asarray(tile, bf16),
        jnp.asarray(mask, f32),
    )

    core = lax.axis_index("aa") % 2
    rows_x = out_x.reshape(8, 2, CHI, 3, CHI).transpose(1, 0, 3, 2, 4).reshape(48, PAIR)
    gram_x = lax.dynamic_slice_in_dim(rows_x, core * 12, 36, 0)
    gram_y = out_y.reshape(8, 3, CHI, 3, CHI).transpose(1, 0, 3, 2, 4).reshape(72, PAIR)
    proj_x = jnp.dot(gram_x, trial_x, precision=HIGHEST, preferred_element_type=jnp.float32)
    proj_y = jnp.dot(gram_y, trial_y, precision=HIGHEST, preferred_element_type=jnp.float32)
    return (gram_x, proj_x, gram_y, proj_y)


def solution(mesh):
    in_specs = (P("aa", "ba", None), P(), P())
    out_specs = (P("aa", None), P("aa", None), P("ba", None), P("ba", None))
    return jax.shard_map(
        per_device, mesh=mesh, in_specs=in_specs, out_specs=out_specs, check_vma=False
    )
```

time: 134 us -> 123 us (0.918)
  Pallas kernels: 128 us -> 117 us
    pallas_call x1, Pallas kernels: 128 us -> 117 us  [per_device(): pl.pallas_call(fused_kernel, out_shape=[jax.ShapeDtypeStruct((16, CHI, 72...]
where the time goes in v4:
time: 123 us; the launch traced here: 122 us
  Pallas kernels  117 us (95%)
  local copies, waits for them, and re-layouts  2.37 us (2%)
  matrix products  1.73 us (1%)
    pallas_call x1, Pallas kernels, per_device(): pl.pallas_call(fused_kernel, out_shape=[jax.ShapeDtypeStruct((16, CHI, 72...  117 us

profile of v4, /device:TPU:1, one launch (start us, length us, event | category | flops | bytes accessed | tf_op | source)
XLA Modules:
  0.0 121.9 jit_solution(372765949071078449)
XLA Ops:
  0.6 0.0 copy-start
  0.7 0.0 copy-start.4
  0.7 117.0 %hotrg_step.1 = (f32[16,24,72]{2,1,0:T(8,128)}, f32[8,3,24,72]{3,2,1,0:T(8,128)}) custom-call(bf16[12,216,576]{2,1,0:T(8,128)(2,1)} %bitcast.14, bf16[256,216]{1,0:T(8,128)(2,1)} %constant.34.clone.ps_ref, bf16[192,192]{1,0:T(8,128)(2,1)} %constant.35.clone.py_ref, bf16[256,256]{1,0:T(8,128)(2,1)} %constant.36.clone.eye_ref, ...), custom_call_target="tpu_custom_call" | custom-call | tf_op jit(solution)/shard_map/hotrg_step/pallas_call | solution.py:650
  117.7 0.0 copy-start.3
  117.7 1.3 %reshape.24 = f32[8,2,24,3,24]{4,3,2,1,0:T(4,128)S(1)} reshape(f32[16,24,72]{2,1,0:T(8,128)} %get-tuple-element.6) | data formatting | bytes 221184 | tf_op jit(solution)/shard_map/reshape | solution.py:692
  119.1 0.2 reshape.25
  119.3 0.0 copy-done.4
  119.3 0.0 copy-start.2
  119.3 0.8 fusion
  120.2 0.0 copy-done.3
  120.2 0.4 reshape.26
  120.6 0.1 copy.15
  120.7 0.3 reshape.27
  121.0 0.0 copy-done
  121.0 0.0 copy-start.1
  121.0 0.9 fusion.1
  121.9 0.0 copy-done.2
  121.9 0.0 copy-done.1
  (2 shorter events, 0.1 us)
Async XLA Ops:
  0.6 120.3 %copy-start = (f32[576,24]{0,1:T(8,128)S(1)}, f32[576,24]{0,1:T(8,128)}, u32[]{:S(2)}) copy-start(f32[576,24]{0,1:T(8,128)} %param.10) | copy-start | bytes 165892
  0.7 118.6 %copy-start.4 = (f32[576,24]{0,1:T(8,128)S(1)}, f32[576,24]{0,1:T(8,128)}, u32[]{:S(2)}) copy-start(f32[576,24]{0,1:T(8,128)} %param.9) | copy-start | bytes 165892
  117.7 2.5 %copy-start.3 = (f32[8,3,24,72]{3,2,1,0:T(8,128)S(1)}, f32[8,3,24,72]{3,2,1,0:T(8,128)}, u32[]{:S(2)}) copy-start(f32[8,3,24,72]{3,2,1,0:T(8,128)} %get-tuple-element.7) | copy-start | bytes 497668
  119.3 2.6 %copy-start.2 = (f32[36,576]{1,0:T(8,128)}, f32[36,576]{1,0:T(8,128)S(1)}, u32[]{:S(2)}) copy-start(f32[36,576]{1,0:T(8,128)S(1)} %constant_dynamic-slice_fusion) | copy-start | bytes 248836
  121.0 0.9 copy-start.1

commit v5 on v4

--- a/solution.py
+++ b/solution.py
@@ -105,17 +105,17 @@
 
 
 def relayout(block, st_ref, mask_ref):
-    spread = jnp.concatenate([block[:, CHI * q : CHI * q + CHI] for q in range(CHI)], axis=0)
-    high = spread.astype(jnp.bfloat16)
-    rest = spread - high.astype(jnp.float32)
-    mid = rest.astype(jnp.bfloat16)
-    low = (rest - mid.astype(jnp.float32)).astype(jnp.bfloat16)
-    st = st_ref[...]
-    tiled = (
-        jnp.dot(high, st, preferred_element_type=jnp.float32)
-        + jnp.dot(mid, st, preferred_element_type=jnp.float32)
-        + jnp.dot(low, st, preferred_element_type=jnp.float32)
+    high = block.astype(jnp.bfloat16).astype(jnp.float32)
+    mid = (block - high).astype(jnp.bfloat16).astype(jnp.float32)
+    terms = (high, mid, block - high - mid)
+    spread = jnp.concatenate(
+        [
+            jnp.concatenate([term[:, CHI * q : CHI * q + CHI] for term in terms], axis=1)
+            for q in range(CHI)
+        ],
+        axis=0,
     )
+    tiled = jnp.dot(spread.astype(jnp.bfloat16), st_ref[...], preferred_element_type=jnp.float32)
     return jnp.sum(tiled.reshape(CHI, CHI, PAIR) * mask_ref[...][None, :, :], axis=1)
 
 
@@ -149,7 +149,7 @@
 
 def fused_kernel(
     t_ref, ps_ref, py_ref, eye_ref, st_ref, mask_ref, ox_ref, oy_ref,
-    snd, got, zbuf, turned, m_up, m_low, q_ref,
+    snd, got, zbuf, turned, m_ref, q_ref,
     send_sem, recv_sem, fsend_sem, frecv_sem,
     parts1, parts2, parts3, sums1, sums2, mine, rows_ab, piece,
     s1_sem, r1_sem, s2_sem, r2_sem, s3_sem, r3_sem, out_sem, rows_sem, x_sem, rx_sem, y_sem, ry_sem,
@@ -205,7 +205,7 @@
 
         return carry
 
-    lax.fori_loop(0, 64, send_to, 0)
+    lax.fori_loop(0, 24, send_to, 0)
 
     two = (i < 4) == (c == 0)
     sibling = (2 * i + (1 - c), j)
@@ -235,6 +235,7 @@
 
         pl.when(two)(lambda: one(2))
         pl.when(jnp.logical_not(two))(lambda: one(1))
+        pl.when(k + 24 < 64)(lambda: send_to(k + 24, None))
         return carry
 
     def accept(k, carry):
@@ -304,100 +305,9 @@
         for z in range(24):
             cols = slice(128 * z, 128 * z + 128)
             straight = [turned[w, 24 * z : 24 * z + 24] for w in range(2)]
-            m_up[half, rows_at, cols] = jnp.concatenate(straight, 0).astype(jnp.bfloat16)
+            m_ref[0, half, rows_at, cols] = jnp.concatenate(straight, 0).astype(jnp.bfloat16)
             strided = [turned[w, pl.ds(z, 24, stride=24)] for w in range(2)]
-            m_low[half, rows_at, cols] = jnp.concatenate(strided, 0).astype(jnp.bfloat16)
-
-    def prepare(legs, half, meanwhile):
-        for n in range(2):
-            @pl.when(c == 0)
-            def _(n=n):
-                at = far(0, legs, n)
-
-                def per_leg(m, carry):
-                    stack_x(6 * at + m, half)
-                    return carry
-
-                lax.fori_loop(0, 6, per_leg, 0)
-
-            @pl.when(c == 1)
-            def _(n=n):
-                at = far(2, legs, n)
-
-                def per_leg(m, carry):
-                    stack_y(2 * at + m, half)
-                    return carry
-
-                lax.fori_loop(0, 2, per_leg, 0)
-
-            at = jnp.where(c == 0, far(0, legs, n), far(2, legs, n))
-
-            def per_pair(m, carry):
-                turn(3 * at + m, half)
-                return carry
-
-            lax.fori_loop(0, 3, per_pair, 0)
-            meanwhile(n)
-
-    panels = ((0, 256), (256, 256), (512, 64))
-
-    def gram(which, m, half):
-        base = PAIR * which
-        for col, width in panels:
-            total = lax.dot_general(
-                m[half, col:, :1536], m[half, col : col + width, :1536],
-                NT, preferred_element_type=jnp.float32,
-            )
-            total += lax.dot_general(
-                m[half, col:, 1536:], m[half, col : col + width, 1536:],
-                NT, preferred_element_type=jnp.float32,
-            )
-            if half:
-                total += q_ref[base + col : base + PAIR, col : col + width]
-            q_ref[base + col : base + PAIR, col : col + width] = total
-            if half and col + width < PAIR:
-                below = q_ref[base + col + width : base + PAIR, col : col + width]
-                q_ref[base + col : base + col + width, col + width :] = below.T
-
-    def passing(start, stop):
-        lax.fori_loop(start, stop, pass_on, 0)
-
-    def accepting(start, stop):
-        lax.fori_loop(start, stop, accept, 0)
-
-    passing(0, 16)
-    accepting(0, 16)
-    prepare(0, 0, lambda n: passing(16 + 8 * n, 24 + 8 * n))
-    accepting(16, 32)
-
-    @pl.when(c == 0)
-    def _():
-        prepare(0, 1, lambda n: passing(32 + 8 * n, 40 + 8 * n))
-
-    @pl.when(c == 1)
-    def _():
-        prepare(1, 0, lambda n: passing(32 + 4 * n, 36 + 4 * n))
-        gram(0, m_up, 0)
-        passing(40, 44)
-        gram(1, m_low, 0)
-        passing(44, 48)
-
-    accepting(32, 48)
-
-    @pl.when(c == 0)
-    def _():
-        prepare(1, 0, lambda n: passing(48 + 4 * n, 52 + 4 * n))
-        gram(0, m_up, 0)
-        passing(56, 60)
-        gram(1, m_low, 0)
-        passing(60, 64)
-
-    @pl.when(c == 1)
-    def _():
-        prepare(0, 1, lambda n: passing(48 + 8 * n, 56 + 8 * n))
-
-    accepting(48, 64)
-    prepare(1, 1, lambda n: None)
+            m_ref[1, half, rows_at, cols] = jnp.concatenate(strided, 0).astype(jnp.bfloat16)
 
     scale = 1.0 / CHI**3
 
@@ -416,13 +326,13 @@
 
             def rows(to, e, part=part):
                 n = jnp.where(c == which, unit_of(part, 0, to, e), unit_of(part, 1, to, e))
-                return pl.ds(pl.multiple_of(PAIR * which + CHI * n, 8), CHI)
+                return pl.ds(pl.multiple_of(CHI * n, 8), CHI)
 
             def send(step, carry, part=part, first=first, at=at, rows=rows):
                 to = (at + step) % 4
                 for e in range(2):
                     pltpu.make_async_remote_copy(
-                        src_ref=q_ref.at[rows(to, e)],
+                        src_ref=q_ref.at[which, rows(to, e)],
                         dst_ref=parts1.at[part, which, at, e],
                         send_sem=s1_sem.at[part, which],
                         recv_sem=r1_sem.at[part, which],
@@ -433,7 +343,86 @@
 
             lax.fori_loop(1, 4, send, 0)
             for e in range(2):
-                parts1[part, which, at, e] = q_ref[rows(at, e)]
+                parts1[part, which, at, e] = q_ref[which, rows(at, e)]
+
+    def passing(start, stop):
+        lax.fori_loop(jnp.minimum(start, 64), jnp.minimum(stop, 64), pass_on, 0)
+
+    def prepare(legs, half, ahead):
+        def per_place(n, carry):
+            at = jnp.where(c == 0, far(0, legs, n), far(2, legs, n))
+
+            @pl.when(c == 0)
+            def _():
+                def per_leg(m, carry):
+                    stack_x(6 * at + m, half)
+                    return carry
+
+                lax.fori_loop(0, 6, per_leg, 0)
+
+            @pl.when(c == 1)
+            def _():
+                def per_leg(m, carry):
+                    stack_y(2 * at + m, half)
+                    return carry
+
+                lax.fori_loop(0, 2, per_leg, 0)
+
+            def per_pair(m, carry):
+                turn(3 * at + m, half)
+                return carry
+
+            lax.fori_loop(0, 3, per_pair, 0)
+            return carry
+
+        lax.fori_loop(0, 2, per_place, 0)
+
+    def gram(which, half):
+        for col, width in ((0, 256), (256, 256), (512, 64)):
+            before = q_ref[which, col:, col : col + width]
+            total = jnp.where(half == 1, before, jnp.zeros_like(before))
+            for ks in (slice(0, 1536), slice(1536, 3072)):
+                total += lax.dot_general(
+                    m_ref[which, half, col:, ks], m_ref[which, half, col : col + width, ks],
+                    NT, preferred_element_type=jnp.float32,
+                )
+            q_ref[which, col:, col : col + width] = total
+
+    def mirror(which):
+        for col, width in ((0, 256), (256, 256)):
+            below = q_ref[which, col + width :, col : col + width]
+            q_ref[which, col : col + width, col + width :] = below.T
+
+    passing(0, 16)
+
+    def quarter(n, carry):
+        ahead = 16 * n + 16
+        lax.fori_loop(16 * n, ahead, accept, 0)
+        near, distant = n % 2, n // 2
+        legs = jnp.where(c == 0, distant, near)
+        half = jnp.where(c == 0, near, distant)
+        prepare(legs, half, ahead)
+        last = n == 3
+        multiplies = jnp.logical_or(last, n == 2 - c)
+
+        @pl.when(multiplies)
+        def _():
+            def one(which, carry):
+                gram(which, half)
+
+                @pl.when(last)
+                def _():
+                    mirror(which)
+                    stage1(which)
+
+                return carry
+
+            lax.fori_loop(0, 2, one, 0)
+
+        passing(ahead, ahead + 16)
+        return carry
+
+    lax.fori_loop(0, 4, quarter, 0)
 
     def stage2(which):
         for part in range(3):
@@ -462,12 +451,11 @@
                 def _(part=part, at=at, e=e):
                     parts2[part, at] = sums1[part, which, e]
 
-    gram(0, m_up, 1)
-    stage1(0)
-    gram(1, m_low, 1)
-    stage1(1)
-    stage2(0)
-    stage2(1)
+    def both(which, carry):
+        stage2(which)
+        return carry
+
+    lax.fori_loop(0, 2, both, 0)
 
     owner = []
     for part in range(3):
@@ -494,12 +482,16 @@
                 device_id_type=MESH,
             ).start()
 
-    for part in range(3):
-        kind, owns = owner[part]
+    def own_part(part, carry):
+        def pick(values):
+            return jnp.where(part == 0, values[0], jnp.where(part == 1, values[1], values[2]))
+
+        kind = pick([jnp.where(k, 1, 0) for k, _ in owner]) == 1
+        owns = pick([jnp.where(o, 1, 0) for _, o in owner]) == 1
         which = jnp.where(kind, 1 - c, c)
 
         @pl.when(owns)
-        def _(part=part, kind=kind, which=which):
+        def _():
             take(parts3.at[part], 3, r3_sem.at[part])
             total = (parts3[part, 0] + parts3[part, 1]) + (parts3[part, 2] + parts3[part, 3])
             mine[part] = relayout(total * scale, st_ref, mask_ref)
@@ -520,6 +512,10 @@
             lax.fori_loop(1, 8, give, 0)
             rows_ab[which, part] = mine[part]
 
+        return carry
+
+    lax.fori_loop(0, 3, own_part, 0)
+
     for part in range(3):
         kind, owns = owner[part]
         for which in range(2):
@@ -604,7 +600,7 @@
             lambda part=part: wait_for(sums2.at[part], s3_sem.at[part])
         )
         pl.when(owns)(
-            lambda part=part: wait_for(q_ref.at[pl.ds(0, 7 * CHI)], out_sem.at[part])
+            lambda part=part: wait_for(q_ref.at[0, pl.ds(0, 7 * CHI)], out_sem.at[part])
         )
 
     lax.fori_loop(0, 64, finish_forward, 0)
@@ -644,7 +640,7 @@
     vmem = pl.BlockSpec(memory_space=pltpu.VMEM)
     dma = pltpu.SemaphoreType.DMA
     index = np.arange(PAIR)
-    tile = (np.arange(CHI)[:, None] == index[None, :] % CHI).astype(np.float32)
+    tile = (np.arange(72)[:, None] % CHI == index[None, :] % CHI).astype(np.float32)
     mask = (np.arange(CHI)[:, None] == index[None, :] // CHI).astype(np.float32)
     f32, bf16 = jnp.float32, jnp.bfloat16
     out_x, out_y = pl.pallas_call(
@@ -660,9 +656,8 @@
             pltpu.VMEM((24, 8, 9, 16, 128), bf16),
             pltpu.VMEM((24, 2, 128, PAIR), bf16),
             pltpu.VMEM((2, PAIR, 128), f32),
-            pltpu.VMEM((2, PAIR, 24 * 128), bf16),
-            pltpu.VMEM((2, PAIR, 24 * 128), bf16),
-            pltpu.VMEM((2 * PAIR, PAIR), f32),
+            pltpu.VMEM((2, 2, PAIR, 24 * 128), bf16),
+            pltpu.VMEM((2, PAIR, PAIR), f32),
             dma((12,)), dma((64,)), dma((64,)), dma((64,)),
             pltpu.VMEM((3, 2, 4, 2, CHI, PAIR), f32),
             pltpu.VMEM((3, 4, CHI, PAIR), f32),

time: 123 us -> 116 us (0.943)
  Pallas kernels: 117 us -> 111 us
    pallas_call x1, Pallas kernels: 117 us -> 111 us  [per_device(): pl.pallas_call(fused_kernel, out_shape=[jax.ShapeDtypeStruct((16, CHI, 72...]
where the time goes in v5:
time: 116 us
  Pallas kernels  111 us (96%)
  local copies, waits for them, and re-layouts  2.37 us (2%)
  matrix products  1.73 us (1%)
    pallas_call x1, Pallas kernels, per_device(): pl.pallas_call(fused_kernel, out_shape=[jax.ShapeDtypeStruct((16, CHI, 72...  111 us

profile of v5, /device:TPU:1, one launch (start us, length us, event | category | flops | bytes accessed | tf_op | source)
XLA Modules:
  0.0 115.7 jit_solution(11215183335237420061)
XLA Ops:
  0.6 0.0 copy-start
  0.7 0.0 copy-start.4
  0.7 110.9 %hotrg_step.1 = (f32[16,24,72]{2,1,0:T(8,128)}, f32[8,3,24,72]{3,2,1,0:T(8,128)}) custom-call(bf16[12,216,576]{2,1,0:T(8,128)(2,1)} %bitcast.14, bf16[256,216]{1,0:T(8,128)(2,1)} %constant.34.clone.ps_ref, bf16[192,192]{1,0:T(8,128)(2,1)} %constant.35.clone.py_ref, bf16[256,256]{1,0:T(8,128)(2,1)} %constant.36.clone.eye_ref, ...), custom_call_target="tpu_custom_call" | custom-call | tf_op jit(solution)/shard_map/hotrg_step/pallas_call | solution.py:646
  111.6 0.0 copy-start.3
  111.6 1.3 %reshape.24 = f32[8,2,24,3,24]{4,3,2,1,0:T(4,128)S(1)} reshape(f32[16,24,72]{2,1,0:T(8,128)} %get-tuple-element.6) | data formatting | bytes 221184 | tf_op jit(solution)/shard_map/reshape | solution.py:687
  112.9 0.2 reshape.25
  113.2 0.0 copy-done.4
  113.2 0.0 copy-start.2
  113.2 0.8 fusion
  114.0 0.0 copy-done.3
  114.0 0.4 reshape.26
  114.5 0.1 copy.15
  114.5 0.3 reshape.27
  114.8 0.0 copy-done
  114.8 0.0 copy-start.1
  114.8 0.9 fusion.1
  115.7 0.0 copy-done.2
  115.7 0.0 copy-done.1
  (2 shorter events, 0.1 us)
Async XLA Ops:
  0.6 114.2 %copy-start = (f32[576,24]{0,1:T(8,128)S(1)}, f32[576,24]{0,1:T(8,128)}, u32[]{:S(2)}) copy-start(f32[576,24]{0,1:T(8,128)} %param.10) | copy-start | bytes 165892
  0.7 112.5 %copy-start.4 = (f32[576,24]{0,1:T(8,128)S(1)}, f32[576,24]{0,1:T(8,128)}, u32[]{:S(2)}) copy-start(f32[576,24]{0,1:T(8,128)} %param.9) | copy-start | bytes 165892
  111.6 2.5 %copy-start.3 = (f32[8,3,24,72]{3,2,1,0:T(8,128)S(1)}, f32[8,3,24,72]{3,2,1,0:T(8,128)}, u32[]{:S(2)}) copy-start(f32[8,3,24,72]{3,2,1,0:T(8,128)} %get-tuple-element.7) | copy-start | bytes 497668
  113.2 2.6 %copy-start.2 = (f32[36,576]{1,0:T(8,128)}, f32[36,576]{1,0:T(8,128)S(1)}, u32[]{:S(2)}) copy-start(f32[36,576]{1,0:T(8,128)S(1)} %constant_dynamic-slice_fusion) | copy-start | bytes 248836
  114.8 0.9 copy-start.1

commit v6 on v5

--- a/solution.py
+++ b/solution.py
@@ -27,6 +27,43 @@
                     h, r = divmod(xs * 9 + y * 3 + ys, 16)
                     out[h * 128 + jd * 16 + r, xs * 72 + y * 24 + jd * 3 + ys] = 1
     return out
+
+
+def tail_slot(r):
+    return (r % 14) // 5, 11 + (r % 14) % 5
+
+
+def send_tails():
+    out = np.zeros((2, 3, 8, 16, 216), np.float32)
+    for jd in range(8):
+        for xs in range(3):
+            for y in range(3):
+                for ys in range(3):
+                    r = xs * 9 + y * 3 + ys
+                    k, row = tail_slot(r)
+                    out[r // 14, k, jd, row, xs * 72 + y * 24 + jd * 3 + ys] = 1
+    return out.reshape(768, 216)
+
+
+def x_tails():
+    out = np.zeros((2, 2, 2, 16, 3, 2, 16), np.float32)
+    for jj in range(2):
+        for r in range(27):
+            k, row = tail_slot(r)
+            out[r // 14, r // 16, jj, r % 16, k, jj, row] = 1
+    return out.reshape(128, 96)
+
+
+def y_tails():
+    out = np.zeros((2, 192, 3, 6, 16), np.float32)
+    for xg in range(6):
+        for xs in range(3):
+            for y in range(3):
+                for ys in range(3):
+                    r = xs * 9 + y * 3 + ys
+                    k, row = tail_slot(r)
+                    out[r // 14, y * 64 + xg * 9 + xs * 3 + ys, k, xg, row] = 1
+    return out.reshape(384, 288)
 
 
 def y_rows():
@@ -148,8 +185,8 @@
 
 
 def fused_kernel(
-    t_ref, ps_ref, py_ref, eye_ref, st_ref, mask_ref, ox_ref, oy_ref,
-    snd, got, zbuf, turned, m_ref, q_ref,
+    t_ref, ps_ref, pt_ref, py_ref, xt_ref, yt_ref, eye_ref, st_ref, mask_ref, ox_ref, oy_ref,
+    unit, load_sem, snd, got, zbuf, turned, m_ref, q_ref,
     send_sem, recv_sem, fsend_sem, frecv_sem,
     parts1, parts2, parts3, sums1, sums2, mine, rows_ab, piece,
     s1_sem, r1_sem, s2_sem, r2_sem, s3_sem, r3_sem, out_sem, rows_sem, x_sem, rx_sem, y_sem, ry_sem,
@@ -160,16 +197,31 @@
     barrier = pltpu.get_barrier_semaphore()
     greet(i, c, j, barrier)
 
+    def load(u):
+        return pltpu.make_async_copy(t_ref.at[u], unit.at[u], load_sem.at[u])
+
+    def start_load(u, carry):
+        load(u).start()
+        return carry
+
+    lax.fori_loop(0, 12, start_load, 0)
+
     def gather_unit(u, carry):
-        rows = jnp.dot(ps_ref[...], t_ref[u], preferred_element_type=jnp.float32)
-        rows = rows.astype(jnp.bfloat16)
-        for h in range(2):
-            for k in range(4):
-                snd[u, :, 4 * h + k] = rows[
-                    128 * h : 128 * h + 128, 128 * k : 128 * k + 128
-                ].reshape(8, 16, 128)
-        last = jnp.concatenate([rows[:128, 512:], rows[128:, 512:]], axis=1)
-        snd[u, :, 8] = last.reshape(8, 16, 128)
+        load(u).wait()
+        rows = jnp.dot(ps_ref[...], unit[u], preferred_element_type=jnp.float32)
+        ends = unit[u, :, 512:]
+        ends = jnp.dot(
+            pt_ref[...], jnp.concatenate([ends, ends], axis=1), preferred_element_type=jnp.float32
+        )
+        left = lax.broadcasted_iota(jnp.int32, (128, 128), 1) < 64
+        for k in range(4):
+            cols = slice(128 * k, 128 * k + 128)
+            second = rows[128:, cols]
+            if k < 3:
+                at = 128 * k
+                second += jnp.where(left, ends[at : at + 128], ends[384 + at : 512 + at])
+            snd[u, :, k] = rows[:128, cols].astype(jnp.bfloat16).reshape(8, 16, 128)
+            snd[u, :, 4 + k] = second.astype(jnp.bfloat16).reshape(8, 16, 128)
         return carry
 
     lax.fori_loop(0, 12, gather_unit, 0)
@@ -205,7 +257,7 @@
 
         return carry
 
-    lax.fori_loop(0, 24, send_to, 0)
+    lax.fori_loop(0, 16, send_to, 0)
 
     two = (i < 4) == (c == 0)
     sibling = (2 * i + (1 - c), j)
@@ -235,7 +287,7 @@
 
         pl.when(two)(lambda: one(2))
         pl.when(jnp.logical_not(two))(lambda: one(1))
-        pl.when(k + 24 < 64)(lambda: send_to(k + 24, None))
+        pl.when(k + 16 < 64)(lambda: send_to(k + 16, None))
         return carry
 
     def accept(k, carry):
@@ -260,15 +312,18 @@
     def stack_x(x, half):
         for n in range(2):
             js = pl.ds(2 * far(2, half, n), 2)
+            tails = jnp.concatenate([got[x, js, 4 + k].reshape(32, 128) for k in range(3)], axis=0)
+            tails = jnp.dot(xt_ref[...], tails, preferred_element_type=jnp.float32)
+            tails = (tails[:64, :64] + tails[64:, 64:]).astype(jnp.bfloat16)
+            used = lax.broadcasted_iota(jnp.int32, (32, 128), 0) % 16 < 11
             for h in range(2):
                 at = slice(64 * h + 32 * n, 64 * h + 32 * n + 32)
                 for k in range(4):
-                    zbuf[x, half, at, 128 * k : 128 * k + 128] = got[x, js, 4 * h + k].reshape(
-                        32, 128
-                    )
-            last = got[x, js, 8].reshape(32, 128)
-            zbuf[x, half, 32 * n : 32 * n + 32, 512:576] = last[:, :64]
-            zbuf[x, half, 64 + 32 * n : 96 + 32 * n, 512:576] = last[:, 64:]
+                    block = got[x, js, 4 * h + k].reshape(32, 128)
+                    if h:
+                        block = jnp.where(used, block, jnp.zeros_like(block))
+                    zbuf[x, half, at, 128 * k : 128 * k + 128] = block
+                zbuf[x, half, at, 512:576] = tails[32 * h : 32 * h + 32]
 
     def stack_y(jd, half):
         for n in range(2):
@@ -283,11 +338,9 @@
                 axis=0,
             )
             rows = jnp.dot(py_ref[...], block, preferred_element_type=jnp.float32)
-            last = got[xs, jd, 8].reshape(96, 128)
-            tail = (
-                jnp.dot(py_ref[:, :96], last, preferred_element_type=jnp.float32)[:, :64]
-                + jnp.dot(py_ref[:, 96:], last, preferred_element_type=jnp.float32)[:, 64:]
-            )
+            tails = jnp.concatenate([got[xs, jd, 4 + k].reshape(96, 128) for k in range(3)], axis=0)
+            tails = jnp.dot(yt_ref[...], tails, preferred_element_type=jnp.float32)
+            tail = tails[:192, :64] + tails[192:, 64:]
             rows = jnp.concatenate([rows, tail], axis=1).astype(jnp.bfloat16)
             for y in range(3):
                 zbuf[3 * jd + y, half, 64 * n : 64 * n + 64] = rows[64 * y : 64 * y + 64]
@@ -649,11 +702,13 @@
             jax.ShapeDtypeStruct((16, CHI, 72), f32),
             jax.ShapeDtypeStruct((8, 3, CHI, 72), f32),
         ],
-        in_specs=[vmem] * 6,
+        in_specs=[pl.BlockSpec(memory_space=pl.ANY)] + [vmem] * 8,
         out_specs=[vmem] * 2,
         scratch_shapes=[
-            pltpu.VMEM((12, 8, 9, 16, 128), bf16),
-            pltpu.VMEM((24, 8, 9, 16, 128), bf16),
+            pltpu.VMEM((12, 216, PAIR), bf16),
+            dma((12,)),
+            pltpu.VMEM((12, 8, 8, 16, 128), bf16),
+            pltpu.VMEM((24, 8, 8, 16, 128), bf16),
             pltpu.VMEM((24, 2, 128, PAIR), bf16),
             pltpu.VMEM((2, PAIR, 128), f32),
             pltpu.VMEM((2, 2, PAIR, 24 * 128), bf16),
@@ -677,7 +732,10 @@
     )(
         tensor.reshape(12, 216, PAIR),
         jnp.asarray(send_rows(), bf16),
+        jnp.asarray(send_tails(), bf16),
         jnp.asarray(y_rows(), bf16),
+        jnp.asarray(x_tails(), bf16),
+        jnp.asarray(y_tails(), bf16),
         jnp.asarray(np.eye(256), bf16),
         jnp.asarray(tile, bf16),
         jnp.asarray(mask, f32),

time: 116 us -> 112 us (0.966); the launches traced: 116 us -> 111 us
  Pallas kernels: 111 us -> 106 us
    pallas_call x1, Pallas kernels: 111 us -> 106 us  [per_device(): pl.pallas_call(fused_kernel, out_shape=[jax.ShapeDtypeStruct((16, CHI, 72...]
where the time goes in v6:
time: 112 us; the launch traced here: 111 us
  Pallas kernels  106 us (95%)
  local copies, waits for them, and re-layouts  2.37 us (2%)
  matrix products  1.73 us (2%)
    pallas_call x1, Pallas kernels, per_device(): pl.pallas_call(fused_kernel, out_shape=[jax.ShapeDtypeStruct((16, CHI, 72...  106 us

profile of v6, /device:TPU:1, one launch (start us, length us, event | category | flops | bytes accessed | tf_op | source)
XLA Modules:
  0.0 110.5 jit_solution(3650205574826516716)
XLA Ops:
  0.6 0.0 copy-start
  0.7 0.0 copy-start.4
  0.7 105.6 %hotrg_step.1 = (f32[16,24,72]{2,1,0:T(8,128)}, f32[8,3,24,72]{3,2,1,0:T(8,128)}) custom-call(bf16[12,216,576]{2,1,0:T(8,128)(2,1)} %bitcast.14, bf16[256,216]{1,0:T(8,128)(2,1)} %constant.40.clone.ps_ref, bf16[768,216]{1,0:T(8,128)(2,1)} %constant.41.clone.pt_ref, bf16[192,192]{1,0:T(8,128)(2,1)} %constant.42.clone.py_ref, ...), custom_call_target="tpu_custom_call" | custom-call | tf_op jit(solution)/shard_map/hotrg_step/pallas_call | solution.py:699
  106.3 0.0 copy-start.3
  106.3 1.3 %reshape.24 = f32[8,2,24,3,24]{4,3,2,1,0:T(4,128)S(1)} reshape(f32[16,24,72]{2,1,0:T(8,128)} %get-tuple-element.6) | data formatting | bytes 221184 | tf_op jit(solution)/shard_map/reshape | solution.py:745
  107.7 0.2 reshape.25
  107.9 0.0 copy-done.4
  107.9 0.0 copy-start.2
  107.9 0.8 fusion
  108.8 0.0 copy-done.3
  108.8 0.4 reshape.26
  109.2 0.1 copy.18
  109.3 0.3 reshape.27
  109.6 0.0 copy-done
  109.6 0.0 copy-start.1
  109.6 0.9 fusion.1
  110.5 0.0 copy-done.2
  110.5 0.0 copy-done.1
  (2 shorter events, 0.1 us)
Async XLA Ops:
  0.6 108.9 %copy-start = (f32[576,24]{0,1:T(8,128)S(1)}, f32[576,24]{0,1:T(8,128)}, u32[]{:S(2)}) copy-start(f32[576,24]{0,1:T(8,128)} %param.13) | copy-start | bytes 165892
  0.7 107.3 %copy-start.4 = (f32[576,24]{0,1:T(8,128)S(1)}, f32[576,24]{0,1:T(8,128)}, u32[]{:S(2)}) copy-start(f32[576,24]{0,1:T(8,128)} %param.12) | copy-start | bytes 165892
  106.3 2.5 %copy-start.3 = (f32[8,3,24,72]{3,2,1,0:T(8,128)S(1)}, f32[8,3,24,72]{3,2,1,0:T(8,128)}, u32[]{:S(2)}) copy-start(f32[8,3,24,72]{3,2,1,0:T(8,128)} %get-tuple-element.7) | copy-start | bytes 497668
  107.9 2.6 %copy-start.2 = (f32[36,576]{1,0:T(8,128)}, f32[36,576]{1,0:T(8,128)S(1)}, u32[]{:S(2)}) copy-start(f32[36,576]{1,0:T(8,128)S(1)} %constant_dynamic-slice_fusion) | copy-start | bytes 248836
  109.6 0.9 copy-start.1

commit v7 on v6

--- a/solution.py
+++ b/solution.py
@@ -283,11 +283,11 @@
             def _():
                 wait_for(ref, recv_sem.at[k])
 
+            pl.when(k + 16 < 64)(lambda: send_to(k + 16, None))
             copy.start()
 
         pl.when(two)(lambda: one(2))
         pl.when(jnp.logical_not(two))(lambda: one(1))
-        pl.when(k + 16 < 64)(lambda: send_to(k + 16, None))
         return carry
 
     def accept(k, carry):
@@ -504,6 +504,16 @@
                 def _(part=part, at=at, e=e):
                     parts2[part, at] = sums1[part, which, e]
 
+    lax.fori_loop(0, 64, finish_forward, 0)
+
+    def drain(u, carry):
+        idest = (12 * c + u) % 8
+        pl.when(idest == i)(lambda: take(snd.at[u], 7, send_sem.at[u]))
+        pl.when(idest != i)(lambda: take(snd.at[u], 8, send_sem.at[u]))
+        return carry
+
+    lax.fori_loop(0, 12, drain, 0)
+
     def both(which, carry):
         stage2(which)
         return carry
@@ -656,15 +666,6 @@
             lambda part=part: wait_for(q_ref.at[0, pl.ds(0, 7 * CHI)], out_sem.at[part])
         )
 
-    lax.fori_loop(0, 64, finish_forward, 0)
-
-    def drain(u, carry):
-        idest = (12 * c + u) % 8
-        pl.when(idest == i)(lambda: take(snd.at[u], 7, send_sem.at[u]))
-        pl.when(idest != i)(lambda: take(snd.at[u], 8, send_sem.at[u]))
-        return carry
-
-    lax.fori_loop(0, 12, drain, 0)
 
     @pl.when(jnp.logical_and(c == 0, j < 4))
     def _():

time: 112 us -> 112 us (level)
  no operation moved by 1% of the time
where the time goes in v7:
time: 112 us; the launch traced here: 111 us
  Pallas kernels  106 us (95%)
  local copies, waits for them, and re-layouts  2.37 us (2%)
  matrix products  1.73 us (2%)
    pallas_call x1, Pallas kernels, per_device(): pl.pallas_call(fused_kernel, out_shape=[jax.ShapeDtypeStruct((16, CHI, 72...  106 us

profile of v7, /device:TPU:1, one launch (start us, length us, event | category | flops | bytes accessed | tf_op | source)
XLA Modules:
  0.0 111.1 jit_solution(553489496172062696)
XLA Ops:
  0.6 0.0 copy-start
  0.7 0.0 copy-start.4
  0.7 106.3 %hotrg_step.1 = (f32[16,24,72]{2,1,0:T(8,128)}, f32[8,3,24,72]{3,2,1,0:T(8,128)}) custom-call(bf16[12,216,576]{2,1,0:T(8,128)(2,1)} %bitcast.14, bf16[256,216]{1,0:T(8,128)(2,1)} %constant.40.clone.ps_ref, bf16[768,216]{1,0:T(8,128)(2,1)} %constant.41.clone.pt_ref, bf16[192,192]{1,0:T(8,128)(2,1)} %constant.42.clone.py_ref, ...), custom_call_target="tpu_custom_call" | custom-call | tf_op jit(solution)/shard_map/hotrg_step/pallas_call | solution.py:700
  106.9 0.0 copy-start.3
  106.9 1.3 %reshape.24 = f32[8,2,24,3,24]{4,3,2,1,0:T(4,128)S(1)} reshape(f32[16,24,72]{2,1,0:T(8,128)} %get-tuple-element.6) | data formatting | bytes 221184 | tf_op jit(solution)/shard_map/reshape | solution.py:746
  108.3 0.2 reshape.25
  108.5 0.0 copy-done.4
  108.5 0.0 copy-start.2
  108.6 0.8 fusion
  109.4 0.0 copy-done.3
  109.4 0.4 reshape.26
  109.8 0.1 copy.18
  109.9 0.3 reshape.27
  110.2 0.0 copy-done
  110.2 0.0 copy-start.1
  110.2 0.9 fusion.1
  111.1 0.0 copy-done.2
  111.1 0.0 copy-done.1
  (2 shorter events, 0.1 us)
Async XLA Ops:
  0.6 109.6 %copy-start = (f32[576,24]{0,1:T(8,128)S(1)}, f32[576,24]{0,1:T(8,128)}, u32[]{:S(2)}) copy-start(f32[576,24]{0,1:T(8,128)} %param.13) | copy-start | bytes 165892
  0.7 107.9 %copy-start.4 = (f32[576,24]{0,1:T(8,128)S(1)}, f32[576,24]{0,1:T(8,128)}, u32[]{:S(2)}) copy-start(f32[576,24]{0,1:T(8,128)} %param.12) | copy-start | bytes 165892
  106.9 2.5 %copy-start.3 = (f32[8,3,24,72]{3,2,1,0:T(8,128)S(1)}, f32[8,3,24,72]{3,2,1,0:T(8,128)}, u32[]{:S(2)}) copy-start(f32[8,3,24,72]{3,2,1,0:T(8,128)} %get-tuple-element.7) | copy-start | bytes 497668
  108.5 2.6 %copy-start.2 = (f32[36,576]{1,0:T(8,128)}, f32[36,576]{1,0:T(8,128)S(1)}, u32[]{:S(2)}) copy-start(f32[36,576]{1,0:T(8,128)S(1)} %constant_dynamic-slice_fusion) | copy-start | bytes 248836
  110.2 0.9 copy-start.1

commit v8 on v7

--- a/solution.py
+++ b/solution.py
@@ -434,7 +434,7 @@
         for col, width in ((0, 256), (256, 256), (512, 64)):
             before = q_ref[which, col:, col : col + width]
             total = jnp.where(half == 1, before, jnp.zeros_like(before))
-            for ks in (slice(0, 1536), slice(1536, 3072)):
+            for ks in (slice(0, 3072),):
                 total += lax.dot_general(
                     m_ref[which, half, col:, ks], m_ref[which, half, col : col + width, ks],
                     NT, preferred_element_type=jnp.float32,

time: 112 us -> 112 us (level)
  no operation moved by 1% of the time
where the time goes in v8:
time: 112 us; the launch traced here: 111 us
  Pallas kernels  106 us (95%)
  local copies, waits for them, and re-layouts  2.37 us (2%)
  matrix products  1.73 us (2%)
    pallas_call x1, Pallas kernels, per_device(): pl.pallas_call(fused_kernel, out_shape=[jax.ShapeDtypeStruct((16, CHI, 72...  106 us

profile of v8, /device:TPU:1, one launch (start us, length us, event | category | flops | bytes accessed | tf_op | source)
XLA Modules:
  0.0 111.1 jit_solution(8316532497169689393)
XLA Ops:
  0.6 0.0 copy-start
  0.7 0.0 copy-start.4
  0.7 106.2 %hotrg_step.1 = (f32[16,24,72]{2,1,0:T(8,128)}, f32[8,3,24,72]{3,2,1,0:T(8,128)}) custom-call(bf16[12,216,576]{2,1,0:T(8,128)(2,1)} %bitcast.14, bf16[256,216]{1,0:T(8,128)(2,1)} %constant.40.clone.ps_ref, bf16[768,216]{1,0:T(8,128)(2,1)} %constant.41.clone.pt_ref, bf16[192,192]{1,0:T(8,128)(2,1)} %constant.42.clone.py_ref, ...), custom_call_target="tpu_custom_call" | custom-call | tf_op jit(solution)/shard_map/hotrg_step/pallas_call | solution.py:700
  106.9 0.0 copy-start.3
  106.9 1.3 %reshape.24 = f32[8,2,24,3,24]{4,3,2,1,0:T(4,128)S(1)} reshape(f32[16,24,72]{2,1,0:T(8,128)} %get-tuple-element.6) | data formatting | bytes 221184 | tf_op jit(solution)/shard_map/reshape | solution.py:746
  108.2 0.2 reshape.25
  108.5 0.0 copy-done.4
  108.5 0.0 copy-start.2
  108.5 0.8 fusion
  109.3 0.0 copy-done.3
  109.3 0.4 reshape.26
  109.8 0.1 copy.18
  109.8 0.3 reshape.27
  110.1 0.0 copy-done
  110.2 0.0 copy-start.1
  110.2 0.9 fusion.1
  111.1 0.0 copy-done.2
  111.1 0.0 copy-done.1
  (2 shorter events, 0.1 us)
Async XLA Ops:
  0.6 109.5 %copy-start = (f32[576,24]{0,1:T(8,128)S(1)}, f32[576,24]{0,1:T(8,128)}, u32[]{:S(2)}) copy-start(f32[576,24]{0,1:T(8,128)} %param.13) | copy-start | bytes 165892
  0.7 107.8 %copy-start.4 = (f32[576,24]{0,1:T(8,128)S(1)}, f32[576,24]{0,1:T(8,128)}, u32[]{:S(2)}) copy-start(f32[576,24]{0,1:T(8,128)} %param.12) | copy-start | bytes 165892
  106.9 2.5 %copy-start.3 = (f32[8,3,24,72]{3,2,1,0:T(8,128)S(1)}, f32[8,3,24,72]{3,2,1,0:T(8,128)}, u32[]{:S(2)}) copy-start(f32[8,3,24,72]{3,2,1,0:T(8,128)} %get-tuple-element.7) | copy-start | bytes 497668
  108.5 2.6 %copy-start.2 = (f32[36,576]{1,0:T(8,128)}, f32[36,576]{1,0:T(8,128)S(1)}, u32[]{:S(2)}) copy-start(f32[36,576]{1,0:T(8,128)S(1)} %constant_dynamic-slice_fusion) | copy-start | bytes 248836
  110.2 0.9 copy-start.1
